TPU v7x, 128 devices: a whole 4x4x4 slice. The times are simulated.
128 devices in a mesh: row: 8 (over z, core), col: 16 (over x, y).
Axes of the slice: x: 4, y: 4, z: 4, core: 2. Of those that a mesh axis runs over, the one named last changes fastest.
Arguments:
- loads: float32 [4, 8, 8, 8, 65536], P(None, None, None, None, ('row', 'col')), may hold values from -5 to 8
- conduct: float32 [8, 8, 8, 65536], P(None, None, None, ('row', 'col')), may hold values from 0.1 to 10
Outputs:
- solution: float32 [4, 8, 8, 8, 65536], P(None, None, None, None, ('row', 'col'))
- residual: float32 [4, 8, 8, 8, 65536], P(None, None, None, None, ('row', 'col'))
- direction: float32 [4, 8, 8, 8, 65536], P(None, None, None, None, ('row', 'col'))
All inputs are finite; a program needn't handle non-finite values.
Results may differ from a plain program's by a relative error of at most 0.00009.
Values sent between devices are 32-bit elements; how exact they have to be, the bound alone decides.
A program may use at most 128 MiB of HBM per device.

v0:
```python
import functools

import jax
import jax.numpy as jnp
import numpy as np
from jax import lax
from jax.experimental import pallas as pl
from jax.experimental.pallas import tpu as pltpu
from jax.sharding import PartitionSpec as P

NODES = 8
SOURCES = 4
LANES = 128
N_ROW = 8
N_COL = 16
SCREENING = 0.5
GLL_INNER = [
    -0.8717401485096066,
    -0.5917001814331423,
    -0.2092992179024789,
    0.2092992179024789,
    0.5917001814331423,
    0.8717401485096066,
]
MESH = pl.DeviceIdType.MESH
FIELD = (2, 2, NODES, NODES, NODES, LANES)
ROWS = 4 * NODES**3


def gll_tables():
    degree = NODES - 1
    points = np.array([-1.0] + GLL_INNER + [1.0])
    previous = points * 0.0 + 1.0
    current = points * 1.0
    for order in range(1, degree):
        following = ((2 * order + 1) * points * current - order * previous) / (order + 1)
        previous = current
        current = following
    weights = 2.0 / (degree * (degree + 1) * current**2)
    spread = points[:, None] - points[None, :]
    index_ids = np.arange(NODES)
    same = index_ids[:, None] == index_ids[None, :]
    safe_spread = np.where(same, 1.0, spread)
    deriv = np.where(same, 0.0, current[:, None] / (current[None, :] * safe_spread))
    corner = degree * (degree + 1) / 4.0
    ends = np.where(index_ids == 0, -corner, np.where(index_ids == degree, corner, 0.0))
    deriv = deriv + np.where(same, ends[None, :], 0.0)
    return deriv, weights


DERIV, WEIGHTS = gll_tables()
SQUARE = DERIV * DERIV
HALF = NODES // 2


def halves(table):
    mirrored = table[:HALF, ::-1][:, :HALF]
    direct = table[:HALF, :HALF]
    plus = (direct + mirrored) / 2.0
    minus = (direct - mirrored) / 2.0
    return plus.tolist(), minus.tolist()


D_PLUS, D_MINUS = halves(DERIV)
Q_PLUS, Q_MINUS = halves(SQUARE)


def fold(values):
    plus = [values[i] + values[7 - i] for i in range(HALF)]
    minus = [values[i] - values[7 - i] for i in range(HALF)]
    return plus, minus


def combine(table, values, transposed):
    out = []
    for a in range(HALF):
        total = None
        for i in range(HALF):
            factor = table[i][a] if transposed else table[a][i]
            term = values[i] * factor
            total = term if total is None else total + term
        out.append(total)
    return out


def unfold(base, turn):
    low = [base[a] + turn[a] for a in range(HALF)]
    high = [base[a] - turn[a] for a in range(HALF)]
    return low + high[::-1]


def derive(values):
    plus, minus = fold(values)
    return unfold(combine(D_MINUS, minus, False), combine(D_PLUS, plus, False))


def derive_back(values):
    plus, minus = fold(values)
    return unfold(combine(D_PLUS, minus, True), combine(D_MINUS, plus, True))


def square_back(values):
    plus, minus = fold(values)
    return unfold(combine(Q_PLUS, plus, True), combine(Q_MINUS, minus, True))


def tile_rows(base):
    return pl.ds(pl.multiple_of(base, 8), 8)


def strided(base):
    return pl.ds(base, 8, stride=8)


def line_x(n):
    base = (n // 8) * 512 + (n % 8) * 8
    return [tile_rows(base + 64 * i) for i in range(NODES)]


def line_y(n):
    return [tile_rows(n * 64 + 8 * j) for j in range(NODES)]


def line_z(n):
    base = pl.multiple_of(n * 64, 64)
    return [strided(base + k) for k in range(NODES)]


def lane_ids():
    return lax.broadcasted_iota(jnp.int32, (8, LANES), 1)


def sum_z(first, last):
    lane = lane_ids()
    total = last + jnp.where(lane < LANES - 1, pltpu.roll(first, LANES - 1, 1), 0.0)
    return jnp.where(lane > 0, pltpu.roll(total, 1, 1), first), total


def solve_kernel(
    loads,
    conduct,
    rhs,
    image,
    inverse,
    scalars,
    flux,
    z0,
    weighted,
    from_x,
    from_y,
    from_edge,
    sums,
    part,
    gather_row,
    gather_col,
    in_sem,
    send_sem,
    recv_sem,
    sum_send,
    sum_recv,
):
    row = lax.axis_index("row")
    col = lax.axis_index("col")
    for ex in range(2):
        for ey in range(2):
            lanes = pl.ds((ex * 2 + ey) * LANES, LANES)
            pltpu.make_async_copy(
                conduct.at[:, :, :, lanes], flux.at[ex, ey], in_sem.at[SOURCES]
            ).start()
    for s in range(SOURCES):
        for ex in range(2):
            for ey in range(2):
                lanes = pl.ds((ex * 2 + ey) * LANES, LANES)
                pltpu.make_async_copy(
                    loads.at[s, :, :, :, lanes], rhs.at[s, ex, ey], in_sem.at[s]
                ).start()

    has_up, has_down = row < N_ROW - 1, row > 0
    has_right, has_left = col < N_COL - 1, col > 0
    ways = [
        (1, 0, has_up),
        (-1, 0, has_down),
        (0, 1, has_right),
        (0, -1, has_left),
        (1, 1, has_up & has_right),
        (1, -1, has_up & has_left),
        (-1, 1, has_down & has_right),
        (-1, -1, has_down & has_left),
    ]
    barrier = pltpu.get_barrier_semaphore()
    for step in range(1, N_ROW):
        pl.semaphore_signal(
            barrier, 1, device_id=(lax.rem(row + step, N_ROW), col), device_id_type=MESH
        )
    for step in range(1, N_COL):
        pl.semaphore_signal(
            barrier, 1, device_id=(row, lax.rem(col + step, N_COL)), device_id_type=MESH
        )
    corners = 0
    for dr, dc, there in ways[4:]:

        @pl.when(there)
        def _():
            pl.semaphore_signal(barrier, 1, device_id=(row + dr, col + dc), device_id_type=MESH)

        corners = corners + there.astype(jnp.int32)

    def transfers(q, ref):
        pieces = [
            (ref.at[1, :, 7], from_x.at[q, 0]),
            (ref.at[0, :, 0], from_x.at[q, 1]),
            (ref.at[:, 1, :, 7], from_y.at[q, 0]),
            (ref.at[:, 0, :, 0], from_y.at[q, 1]),
            (ref.at[1, 1, 7, 7], from_edge.at[q, 0]),
            (ref.at[1, 0, 7, 0], from_edge.at[q, 1]),
            (ref.at[0, 1, 0, 7], from_edge.at[q, 2]),
            (ref.at[0, 0, 0, 0], from_edge.at[q, 3]),
        ]
        return [
            pltpu.make_async_remote_copy(
                src,
                dst,
                send_sem.at[q, n],
                recv_sem.at[q, n],
                device_id=(row + ways[n][0], col + ways[n][1]),
                device_id_type=MESH,
            )
            for n, (src, dst) in enumerate(pieces)
        ]

    order = (2, 3, 0, 1, 4, 5, 6, 7)

    def send(q, ref):
        copies = transfers(q, ref)
        for n in order:

            @pl.when(ways[n][2])
            def _():
                copies[n].start()

    def finish(q, ref):
        copies = transfers(q, ref)
        for n in order:

            @pl.when(ways[n][2])
            def _():
                copies[n].wait_send()

        for n in order:

            @pl.when(ways[n ^ 1 if n < 4 else 11 - n][2])
            def _():
                copies[n].wait_recv()

    def clear(ref, there, pick):
        @pl.when(jnp.logical_not(there))
        def _():
            def body(q, carry):
                target = pick(ref, q)
                target[...] = jnp.zeros_like(target)
                return carry

            lax.fori_loop(0, 9, body, 0)

    clear(from_x, has_down, lambda ref, q: ref.at[q, 0])
    clear(from_x, has_up, lambda ref, q: ref.at[q, 1])
    clear(from_y, has_left, lambda ref, q: ref.at[q, 0])
    clear(from_y, has_right, lambda ref, q: ref.at[q, 1])
    clear(from_edge, has_down & has_left, lambda ref, q: ref.at[q, 0])
    clear(from_edge, has_down & has_right, lambda ref, q: ref.at[q, 1])
    clear(from_edge, has_up & has_left, lambda ref, q: ref.at[q, 2])
    clear(from_edge, has_up & has_right, lambda ref, q: ref.at[q, 3])
    sums[...] = jnp.zeros_like(sums)

    def assemble(q, ref):
        def along_x(j, carry):
            for ey in range(2):
                ref[0, ey, 0, j] = ref[0, ey, 0, j] + from_x[q, 0, ey, j]
                ref[1, ey, 7, j] = ref[1, ey, 7, j] + from_x[q, 1, ey, j]
                both = ref[0, ey, 7, j] + ref[1, ey, 0, j]
                ref[0, ey, 7, j] = both
                ref[1, ey, 0, j] = both
            return carry

        lax.fori_loop(0, NODES, along_x, 0, unroll=4)
        for side in range(2):
            from_y[q, side, 0, 0] = from_y[q, side, 0, 0] + from_edge[q, side]
            from_y[q, side, 1, 7] = from_y[q, side, 1, 7] + from_edge[q, 2 + side]
            both = from_y[q, side, 0, 7] + from_y[q, side, 1, 0]
            from_y[q, side, 0, 7] = both
            from_y[q, side, 1, 0] = both

        def along_y(i, carry):
            for ex in range(2):
                ref[ex, 0, i, 0] = ref[ex, 0, i, 0] + from_y[q, 0, ex, i]
                ref[ex, 1, i, 7] = ref[ex, 1, i, 7] + from_y[q, 1, ex, i]
                both = ref[ex, 0, i, 7] + ref[ex, 1, i, 0]
                ref[ex, 0, i, 7] = both
                ref[ex, 1, i, 0] = both
            return carry

        lax.fori_loop(0, NODES, along_y, 0, unroll=4)

    def along_z(flat):
        def body(n, carry):
            base = pl.multiple_of(n * 64, 64)
            first, last = sum_z(flat[strided(base), :], flat[strided(base + 7), :])
            flat[strided(base), :] = first
            flat[strided(base + 7), :] = last
            return carry

        lax.fori_loop(0, 32, body, 0, unroll=8)

    flux2 = flux.reshape(ROWS, LANES)
    inverse2 = inverse.reshape(ROWS, LANES)
    weighted2 = weighted.reshape(ROWS, LANES)
    z02 = z0.reshape(ROWS, LANES)

    pltpu.make_async_copy(flux, flux, in_sem.at[SOURCES]).wait()
    node = lax.broadcasted_iota(jnp.int32, (8, LANES), 0)
    weight_z = jnp.full((8, LANES), WEIGHTS[3], jnp.float32)
    for k in (0, 1, 2):
        ends = (node == k) | (node == 7 - k)
        weight_z = jnp.where(ends, jnp.float32(WEIGHTS[k]), weight_z)

    def weigh(t, carry):
        for i in range(NODES):
            for j in range(NODES):
                at = tile_rows(t * 512 + i * 64 + j * 8)
                flux2[at, :] = flux2[at, :] * (weight_z * float(WEIGHTS[i] * WEIGHTS[j]))
        return carry

    lax.fori_loop(0, 4, weigh, 0)

    def diag_x(n, carry):
        at = line_x(n)
        values = [flux2[a, :] for a in at]
        for a, v, r in zip(at, values, square_back(values)):
            inverse2[a, :] = r + SCREENING * v
        return carry

    def diag_y(n, carry):
        at = line_y(n)
        result = square_back([flux2[a, :] for a in at])
        for a, r in zip(at, result):
            inverse2[a, :] = inverse2[a, :] + r
        return carry

    def diag_z(n, carry):
        at = line_z(n)
        result = square_back([flux2[a, :] for a in at])
        for a, r in zip(at, result):
            inverse2[a, :] = inverse2[a, :] + r
        return carry

    lax.fori_loop(0, 32, diag_x, 0, unroll=2)
    lax.fori_loop(0, 32, diag_y, 0, unroll=2)
    lax.fori_loop(0, 32, diag_z, 0, unroll=2)

    pl.semaphore_wait(barrier, N_ROW - 1 + N_COL - 1 + corners)

    def arrive(s):
        pltpu.make_async_copy(rhs.at[s], rhs.at[s], in_sem.at[s]).wait()
        send(s, rhs.at[s])

    arrive(0)
    send(SOURCES, inverse)
    arrive(1)
    finish(SOURCES, inverse)
    assemble(SOURCES, inverse)
    along_z(inverse2)

    lane = lane_ids()
    twice_z = ((node == 0) & (lane > 0)) | ((node == 7) & (lane < LANES - 1))
    share_z = jnp.where(twice_z, jnp.float32(0.5), jnp.float32(1.0))

    def invert(n, carry):
        for j in range(NODES):
            at = tile_rows(n * 64 + 8 * j)
            value = 1.0 / inverse2[at, :]
            inverse2[at, :] = value
            weighted2[at, :] = value * share_z
        return carry

    lax.fori_loop(0, 32, invert, 0)
    shares = [
        (has_down, 0, 0),
        (None, 0, 7),
        (None, 1, 0),
        (has_up, 1, 7),
    ]
    for there, ex, i in shares:
        share = 0.5 if there is None else jnp.where(there, 0.5, 1.0).astype(jnp.float32)
        for ey in range(2):
            weighted[ex, ey, i] = weighted[ex, ey, i] * share
    shares = [
        (has_left, 0, 0),
        (None, 0, 7),
        (None, 1, 0),
        (has_right, 1, 7),
    ]
    for there, ey, j in shares:
        share = 0.5 if there is None else jnp.where(there, 0.5, 1.0).astype(jnp.float32)
        for ex in range(2):
            weighted[ex, ey, :, j] = weighted[ex, ey, :, j] * share

    zero = jnp.zeros((8, LANES), jnp.float32)

    def put_sum(at, value):
        sums[pl.ds(at, 1), :] = jnp.sum(value, axis=0, keepdims=True)

    def settle(s):
        finish(SOURCES + 1 + s, image.at[s])
        assemble(SOURCES + 1 + s, image.at[s])
        flat = image.at[s].reshape(ROWS, LANES)

        def body(n, carry):
            for j in range(NODES):
                at = tile_rows(n * 64 + 8 * j)
                value = flat[at, :]
                carry = carry + value * value * weighted2[at, :]
            return carry

        put_sum(8 + s, lax.fori_loop(0, 32, body, zero))

    def source(s, carry):
        finish(s, rhs.at[s])
        assemble(s, rhs.at[s])
        right = rhs.at[s].reshape(ROWS, LANES)
        flat = image.at[s].reshape(ROWS, LANES)
        along_z(right)

        def scale(n, carry):
            for j in range(NODES):
                at = tile_rows(n * 64 + 8 * j)
                value = right[at, :]
                z02[at, :] = value * inverse2[at, :]
                carry = carry + value * value * weighted2[at, :]
            return carry

        put_sum(s, lax.fori_loop(0, 32, scale, zero))

        def stiff(at):
            values = [z02[a, :] for a in at]
            weight = [flux2[a, :] for a in at]
            slopes = [g * w for g, w in zip(derive(values), weight)]
            return values, weight, derive_back(slopes)

        def stiff_x(n, carry):
            at = line_x(n)
            values, weight, result = stiff(at)
            for a, v, w, r in zip(at, values, weight, result):
                flat[a, :] = r + SCREENING * w * v
            return carry

        def stiff_y(n, carry):
            at = line_y(n)
            _, _, result = stiff(at)
            for a, r in zip(at, result):
                flat[a, :] = flat[a, :] + r
            return carry

        def stiff_z(n, carry):
            at = line_z(n)
            values, _, result = stiff(at)
            result = [flat[a, :] + r for a, r in zip(at, result)]
            for v, r in zip(values, result):
                carry = carry + v * r
            result[0], result[7] = sum_z(result[0], result[7])
            for a, r in zip(at, result):
                flat[a, :] = r
            return carry

        lax.fori_loop(0, 32, stiff_x, 0, unroll=2)
        lax.fori_loop(0, 32, stiff_y, 0, unroll=2)
        put_sum(4 + s, lax.fori_loop(0, 32, stiff_z, zero, unroll=2))
        send(SOURCES + 1 + s, image.at[s])

        @pl.when(s < SOURCES - 2)
        def _():
            arrive(s + 2)

        @pl.when(s > 0)
        def _():
            settle(s - 1)

        return carry

    lax.fori_loop(0, SOURCES, source, 0)
    settle(SOURCES - 1)

    def gather(stage, slots, mine, count, at, target):
        slots[at] = mine[...]
        copies = [
            pltpu.make_async_remote_copy(
                mine,
                slots.at[at],
                sum_send.at[stage],
                sum_recv.at[stage],
                device_id=target(lax.rem(at + step, count)),
                device_id_type=MESH,
            )
            for step in range(1, count)
        ]
        for copy in copies:
            copy.start()
        others = slots.at[pl.ds(0, count - 1)]
        pltpu.make_async_copy(others, others, sum_recv.at[stage]).wait()
        pltpu.make_async_copy(others, others, sum_send.at[stage]).wait()
        total = slots[0]
        for n in range(1, count):
            total = total + slots[n]
        return total

    part[...] = gather(0, gather_row, sums, N_ROW, row, lambda r: (r, col))
    total = gather(1, gather_col, part, N_COL, col, lambda c: (row, c))
    total = jnp.sum(total, axis=1, keepdims=True)
    rz_first, curvature, square = total[0:4], total[4:8], total[8:12]
    alpha = rz_first / curvature
    rz_second = alpha * alpha * square - rz_first
    beta = rz_second / rz_first
    scalars[0:4, :] = jnp.broadcast_to(alpha, (4, LANES))
    scalars[4:8, :] = jnp.broadcast_to(beta, (4, LANES))


def update_kernel(rhs, image, inverse, scalars, solution_out, residual_out, direction_out):
    s = pl.program_id(0)
    i = pl.program_id(1)
    alpha = jnp.broadcast_to(scalars[pl.ds(s, 1), :], (8, LANES))
    beta = jnp.broadcast_to(scalars[pl.ds(s + 4, 1), :], (8, LANES))
    for ex in range(2):
        for ey in range(2):
            lanes = pl.ds((ex * 2 + ey) * LANES, LANES)
            for j in range(NODES):
                right = rhs[s, ex, ey, i, j]
                inv = inverse[ex, ey, i, j]
                rest = right - alpha * image[s, ex, ey, i, j]
                solution_out[0, 0, j, :, lanes] = alpha * (right * inv)
                residual_out[0, 0, j, :, lanes] = rest
                direction_out[0, 0, j, :, lanes] = (rest + beta * right) * inv


def per_device(loads, conduct):
    f32 = jnp.float32
    vmem = pltpu.VMEM
    whole = pl.BlockSpec(memory_space=vmem)
    many = (SOURCES,) + FIELD
    rhs, image, inverse, scalars = pl.pallas_call(
        solve_kernel,
        out_shape=[vmem(many, f32), vmem(many, f32), vmem(FIELD, f32), vmem((8, LANES), f32)],
        in_specs=[pl.BlockSpec(memory_space=pl.ANY)] * 2,
        out_specs=[whole] * 4,
        scratch_shapes=[
            vmem(FIELD, f32),
            vmem(FIELD, f32),
            vmem(FIELD, f32),
            vmem((9, 2, 2, NODES, NODES, LANES), f32),
            vmem((9, 2, 2, NODES, NODES, LANES), f32),
            vmem((9, 4, NODES, LANES), f32),
            vmem((16, LANES), f32),
            vmem((16, LANES), f32),
            vmem((N_ROW, 16, LANES), f32),
            vmem((N_COL, 16, LANES), f32),
            pltpu.SemaphoreType.DMA((SOURCES + 1,)),
            pltpu.SemaphoreType.DMA((9, 8)),
            pltpu.SemaphoreType.DMA((9, 8)),
            pltpu.SemaphoreType.DMA((2,)),
            pltpu.SemaphoreType.DMA((2,)),
        ],
        compiler_params=pltpu.CompilerParams(
            collective_id=0, has_side_effects=True, vmem_limit_bytes=40 * 1024 * 1024
        ),
    )(loads, conduct)
    shape = (SOURCES, NODES, NODES, NODES, 4 * LANES)
    block = pl.BlockSpec((1, 1, NODES, NODES, 4 * LANES), lambda s, i: (s, i, 0, 0, 0))
    return pl.pallas_call(
        update_kernel,
        grid=(SOURCES, NODES),
        out_shape=[jax.ShapeDtypeStruct(shape, f32)] * 3,
        in_specs=[whole] * 4,
        out_specs=[block] * 3,
        compiler_params=pltpu.CompilerParams(vmem_limit_bytes=16 * 1024 * 1024),
    )(*[pltpu.with_memory_space_constraint(x, vmem) for x in (rhs, image, inverse, scalars)])


def solution(mesh):
    in_specs = (P(None, None, None, None, ("row", "col")), P(None, None, None, ("row", "col")))
    out = P(None, None, None, None, ("row", "col"))
    return jax.shard_map(
        per_device, mesh=mesh, in_specs=in_specs, out_specs=(out, out, out), check_vma=False
    )
```

profile of v0, /device:TPU:1, one launch (start us, length us, event | category | flops | bytes accessed | tf_op | source)
XLA Modules:
  0.0 70.4 jit_solution(12006574997011960450)
XLA Ops:
  0.6 0.0 copy-start
  0.6 1.2 %copy-done = f32[8,8,8,512]{3,2,1,0:T(8,128)S(1)} copy-done((f32[8,8,8,512]{3,2,1,0:T(8,128)S(1)}, f32[8,8,8,512]{3,2,1,0:T(8,128)}, u32[]{:S(2)}) %copy-start) | copy-done | bytes 1048600
  1.9 56.2 %shard_map.49 = (f32[4,2,2,8,8,8,128]{6,5,4,3,2,1,0:T(8,128)S(1)}, f32[4,2,2,8,8,8,128]{6,5,4,3,2,1,0:T(8,128)S(1)}, f32[2,2,8,8,8,128]{5,4,3,2,1,0:T(8,128)S(1)}, f32[8,128]{1,0:T(8,128)S(1)}) custom-call(f32[4,8,8,8,512]{4,3,2,1,0:T(8,128)} %loads.1, f32[8,8,8,512]{3,2,1,0:T(8,128)S(1)} %copy-done), custom_call_target="tpu_custom_call" | custom-call | tf_op jit(solution)/shard_map/pallas_call | solution.py:548
  58.0 12.3 %shard_map.50 = (f32[4,8,8,8,512]{4,3,2,1,0:T(8,128)}, f32[4,8,8,8,512]{4,3,2,1,0:T(8,128)}, f32[4,8,8,8,512]{4,3,2,1,0:T(8,128)}) custom-call(f32[4,2,2,8,8,8,128]{6,5,4,3,2,1,0:T(8,128)S(1)} %get-tuple-element.7.rhs, f32[4,2,2,8,8,8,128]{6,5,4,3,2,1,0:T(8,128)S(1)} %get-tuple-element.8.image, f32[2,2,8,8,8,128]{5,4,3,2,1,0:T(8,128)S(1)} %get-tuple-element.9.inverse, ...), custom_call_target="tpu_custom_call" | custom-call | tf_op jit(solution)/shard_map/pallas_call | solution.py:576
Async XLA Ops:
  0.6 1.2 %copy-start = (f32[8,8,8,512]{3,2,1,0:T(8,128)S(1)}, f32[8,8,8,512]{3,2,1,0:T(8,128)}, u32[]{:S(2)}) copy-start(f32[8,8,8,512]{3,2,1,0:T(8,128)} %conduct.1) | copy-start | bytes 3145732
where the time goes:
time: 70.5 us; the launch traced here: 70.4 us
  Pallas kernels  68.5 us (97%)
  local copies, waits for them, and re-layouts  1.22 us (2%)
    pallas_call x1, Pallas kernels, per_device(): pl.pallas_call(solve_kernel, out_shape=[vmem(many, f32), vmem(many, f32),...  56.2 us
    pallas_call x1, Pallas kernels, per_device(): pl.pallas_call(update_kernel, grid=(SOURCES, NODES), out_shape=[jax.Shape...  12.3 us

commit v1 on v0

--- a/solution.py
+++ b/solution.py
@@ -61,8 +61,8 @@
     return plus.tolist(), minus.tolist()
 
 
-D_PLUS, D_MINUS = halves(DERIV)
-Q_PLUS, Q_MINUS = halves(SQUARE)
+D_PLUS, D_MINUS = halves(DERIV * np.sqrt(2.0))
+Q_PLUS, Q_MINUS = halves(SQUARE * 2.0)
 
 
 def fold(values):
@@ -144,6 +144,8 @@
     inverse,
     scalars,
     flux,
+    flux_z,
+    part_z,
     z0,
     weighted,
     from_x,
@@ -327,7 +329,7 @@
         for i in range(NODES):
             for j in range(NODES):
                 at = tile_rows(t * 512 + i * 64 + j * 8)
-                flux2[at, :] = flux2[at, :] * (weight_z * float(WEIGHTS[i] * WEIGHTS[j]))
+                flux2[at, :] = flux2[at, :] * (weight_z * float(SCREENING * WEIGHTS[i] * WEIGHTS[j]))
         return carry
 
     lax.fori_loop(0, 4, weigh, 0)
@@ -336,7 +338,7 @@
         at = line_x(n)
         values = [flux2[a, :] for a in at]
         for a, v, r in zip(at, values, square_back(values)):
-            inverse2[a, :] = r + SCREENING * v
+            inverse2[a, :] = r + v
         return carry
 
     def diag_y(n, carry):
@@ -348,9 +350,12 @@
 
     def diag_z(n, carry):
         at = line_z(n)
-        result = square_back([flux2[a, :] for a in at])
-        for a, r in zip(at, result):
-            inverse2[a, :] = inverse2[a, :] + r
+        values = [flux2[a, :] for a in at]
+        before = [inverse2[a, :] for a in at]
+        for a, v in zip(line_y(n), values):
+            flux_z[a, :] = v
+        for a, b, r in zip(at, before, square_back(values)):
+            inverse2[a, :] = b + r
         return carry
 
     lax.fori_loop(0, 32, diag_x, 0, unroll=2)
@@ -365,7 +370,8 @@
 
     arrive(0)
     send(SOURCES, inverse)
-    arrive(1)
+    for s in range(1, SOURCES):
+        arrive(s)
     finish(SOURCES, inverse)
     assemble(SOURCES, inverse)
     along_z(inverse2)
@@ -413,6 +419,7 @@
         finish(SOURCES + 1 + s, image.at[s])
         assemble(SOURCES + 1 + s, image.at[s])
         flat = image.at[s].reshape(ROWS, LANES)
+        along_z(flat)
 
         def body(n, carry):
             for j in range(NODES):
@@ -440,53 +447,51 @@
 
         put_sum(s, lax.fori_loop(0, 32, scale, zero))
 
-        def stiff(at):
+        def stiff(at, weight):
             values = [z02[a, :] for a in at]
-            weight = [flux2[a, :] for a in at]
             slopes = [g * w for g, w in zip(derive(values), weight)]
-            return values, weight, derive_back(slopes)
+            return values, derive_back(slopes)
 
         def stiff_x(n, carry):
             at = line_x(n)
-            values, weight, result = stiff(at)
+            weight = [flux2[a, :] for a in at]
+            values, result = stiff(at, weight)
             for a, v, w, r in zip(at, values, weight, result):
-                flat[a, :] = r + SCREENING * w * v
-            return carry
-
-        def stiff_y(n, carry):
+                flat[a, :] = r + w * v
+            return carry
+
+        def stiff_yz(n, carry):
             at = line_y(n)
-            _, _, result = stiff(at)
-            for a, r in zip(at, result):
-                flat[a, :] = flat[a, :] + r
-            return carry
-
-        def stiff_z(n, carry):
-            at = line_z(n)
-            values, _, result = stiff(at)
-            result = [flat[a, :] + r for a, r in zip(at, result)]
-            for v, r in zip(values, result):
-                carry = carry + v * r
-            result[0], result[7] = sum_z(result[0], result[7])
-            for a, r in zip(at, result):
-                flat[a, :] = r
-            return carry
-
-        lax.fori_loop(0, 32, stiff_x, 0, unroll=2)
-        lax.fori_loop(0, 32, stiff_y, 0, unroll=2)
-        put_sum(4 + s, lax.fori_loop(0, 32, stiff_z, zero, unroll=2))
+            strips = line_z(n)
+            before = [flat[a, :] for a in at]
+            _, result_y = stiff(at, [flux2[a, :] for a in at])
+            _, result_z = stiff(strips, [flux_z[a, :] for a in at])
+            for a, r in zip(strips, result_z):
+                part_z[a, :] = r
+            for a, b, r in zip(at, before, result_y):
+                flat[a, :] = b + r
+            return carry
+
+        def add_z(n, carry):
+            for a in line_y(n):
+                total = flat[a, :] + part_z[a, :]
+                flat[a, :] = total
+                carry = carry + z02[a, :] * total
+            return carry
+
+        lax.fori_loop(0, 32, stiff_x, 0, unroll=4)
+        lax.fori_loop(0, 32, stiff_yz, 0, unroll=2)
+        put_sum(4 + s, lax.fori_loop(0, 32, add_z, zero, unroll=2))
         send(SOURCES + 1 + s, image.at[s])
 
-        @pl.when(s < SOURCES - 2)
+        @pl.when(s > 1)
         def _():
-            arrive(s + 2)
-
-        @pl.when(s > 0)
-        def _():
-            settle(s - 1)
+            settle(s - 2)
 
         return carry
 
     lax.fori_loop(0, SOURCES, source, 0)
+    settle(SOURCES - 2)
     settle(SOURCES - 1)
 
     def gather(stage, slots, mine, count, at, target):
@@ -512,9 +517,15 @@
             total = total + slots[n]
         return total
 
-    part[...] = gather(0, gather_row, sums, N_ROW, row, lambda r: (r, col))
-    total = gather(1, gather_col, part, N_COL, col, lambda c: (row, c))
-    total = jnp.sum(total, axis=1, keepdims=True)
+    total = jnp.sum(sums[...], axis=1, keepdims=True)
+    node16 = lax.broadcasted_iota(jnp.int32, (16, LANES), 0)
+    lane16 = lax.broadcasted_iota(jnp.int32, (16, LANES), 1)
+    packed = jnp.where(node16 == lane16, jnp.broadcast_to(total, (16, LANES)), 0.0)
+    part[0:1, :] = jnp.sum(packed, axis=0, keepdims=True)
+    part[1:2, :] = gather(0, gather_row, part.at[0:1], N_ROW, row, lambda r: (r, col))
+    total = gather(1, gather_col, part.at[1:2], N_COL, col, lambda c: (row, c))
+    total = jnp.broadcast_to(total, (16, LANES))
+    total = jnp.sum(jnp.where(node16 == lane16, total, 0.0), axis=1, keepdims=True)
     rz_first, curvature, square = total[0:4], total[4:8], total[8:12]
     alpha = rz_first / curvature
     rz_second = alpha * alpha * square - rz_first
@@ -523,21 +534,49 @@
     scalars[4:8, :] = jnp.broadcast_to(beta, (4, LANES))
 
 
-def update_kernel(rhs, image, inverse, scalars, solution_out, residual_out, direction_out):
-    s = pl.program_id(0)
-    i = pl.program_id(1)
-    alpha = jnp.broadcast_to(scalars[pl.ds(s, 1), :], (8, LANES))
-    beta = jnp.broadcast_to(scalars[pl.ds(s + 4, 1), :], (8, LANES))
-    for ex in range(2):
-        for ey in range(2):
-            lanes = pl.ds((ex * 2 + ey) * LANES, LANES)
-            for j in range(NODES):
-                right = rhs[s, ex, ey, i, j]
-                inv = inverse[ex, ey, i, j]
-                rest = right - alpha * image[s, ex, ey, i, j]
-                solution_out[0, 0, j, :, lanes] = alpha * (right * inv)
-                residual_out[0, 0, j, :, lanes] = rest
-                direction_out[0, 0, j, :, lanes] = (rest + beta * right) * inv
+SLOTS = 8
+
+
+def update_kernel(rhs, image, inverse, scalars, first, second, third, staging, sem):
+    outputs = (first, second, third)
+
+    def copies(n):
+        return [
+            pltpu.make_async_copy(
+                staging.at[n % SLOTS, q], outputs[q].at[n // NODES, n % NODES], sem.at[n % SLOTS, q]
+            )
+            for q in range(3)
+        ]
+
+    def step(n, carry):
+        s, i, slot = n // NODES, n % NODES, n % SLOTS
+
+        @pl.when(n >= SLOTS)
+        def _():
+            for copy in copies(n - SLOTS):
+                copy.wait()
+
+        alpha = jnp.broadcast_to(scalars[pl.ds(s, 1), :], (8, LANES))
+        beta = jnp.broadcast_to(scalars[pl.ds(s + 4, 1), :], (8, LANES))
+        for ex in range(2):
+            for ey in range(2):
+                lanes = pl.ds((ex * 2 + ey) * LANES, LANES)
+                for j in range(NODES):
+                    right = rhs[s, ex, ey, i, j]
+                    inv = inverse[ex, ey, i, j]
+                    rest = right - alpha * image[s, ex, ey, i, j]
+                    staging[slot, 0, j, :, lanes] = alpha * (right * inv)
+                    staging[slot, 1, j, :, lanes] = rest
+                    staging[slot, 2, j, :, lanes] = (rest + beta * right) * inv
+        for copy in copies(n):
+            copy.start()
+        return carry
+
+    steps = SOURCES * NODES
+    lax.fori_loop(0, steps, step, 0)
+    for n in range(steps - SLOTS, steps):
+        for copy in copies(n):
+            copy.wait()
 
 
 def per_device(loads, conduct):
@@ -552,15 +591,17 @@
         out_specs=[whole] * 4,
         scratch_shapes=[
             vmem(FIELD, f32),
+            vmem((ROWS, LANES), f32),
+            vmem((ROWS, LANES), f32),
             vmem(FIELD, f32),
             vmem(FIELD, f32),
             vmem((9, 2, 2, NODES, NODES, LANES), f32),
             vmem((9, 2, 2, NODES, NODES, LANES), f32),
             vmem((9, 4, NODES, LANES), f32),
             vmem((16, LANES), f32),
-            vmem((16, LANES), f32),
-            vmem((N_ROW, 16, LANES), f32),
-            vmem((N_COL, 16, LANES), f32),
+            vmem((8, LANES), f32),
+            vmem((N_ROW, 1, LANES), f32),
+            vmem((N_COL, 1, LANES), f32),
             pltpu.SemaphoreType.DMA((SOURCES + 1,)),
             pltpu.SemaphoreType.DMA((9, 8)),
             pltpu.SemaphoreType.DMA((9, 8)),
@@ -570,15 +611,17 @@
         compiler_params=pltpu.CompilerParams(
             collective_id=0, has_side_effects=True, vmem_limit_bytes=40 * 1024 * 1024
         ),
-    )(loads, conduct)
+    )(*[pltpu.with_memory_space_constraint(x, pltpu.HBM) for x in (loads, conduct)])
     shape = (SOURCES, NODES, NODES, NODES, 4 * LANES)
-    block = pl.BlockSpec((1, 1, NODES, NODES, 4 * LANES), lambda s, i: (s, i, 0, 0, 0))
     return pl.pallas_call(
         update_kernel,
-        grid=(SOURCES, NODES),
         out_shape=[jax.ShapeDtypeStruct(shape, f32)] * 3,
         in_specs=[whole] * 4,
-        out_specs=[block] * 3,
+        out_specs=[pl.BlockSpec(memory_space=pl.ANY)] * 3,
+        scratch_shapes=[
+            vmem((SLOTS, 3, NODES, NODES, 4 * LANES), f32),
+            pltpu.SemaphoreType.DMA((SLOTS, 3)),
+        ],
         compiler_params=pltpu.CompilerParams(vmem_limit_bytes=16 * 1024 * 1024),
     )(*[pltpu.with_memory_space_constraint(x, vmem) for x in (rhs, image, inverse, scalars)])
 

time: 70.5 us -> 54.1 us (0.77)
  Pallas kernels: 68.5 us -> 53.2 us
  local copies, waits for them, and re-layouts: 1.22 us -> 0 us
    pallas_call x1, Pallas kernels: 56.2 us -> 48.4 us  [per_device(): pl.pallas_call(solve_kernel, out_shape=[vmem(many, f32), vmem(many, f32),...]
    pallas_call x1, Pallas kernels: 12.3 us -> 4.76 us  [per_device(): pl.pallas_call(update_kernel, out_shape=[jax.ShapeDtypeStruct(shape, f32)...]
    unnamed x2 -> x0, local copies, waits for them, and re-layouts: 1.22 us -> none
where the time goes in v1:
time: 54.1 us; the launch traced here: 53.8 us
  Pallas kernels  53.2 us (98%)
  between operations  0.64 us (1%)
    pallas_call x1, Pallas kernels, per_device(): pl.pallas_call(solve_kernel, out_shape=[vmem(many, f32), vmem(many, f32),...  48.4 us
    pallas_call x1, Pallas kernels, per_device(): pl.pallas_call(update_kernel, out_shape=[jax.ShapeDtypeStruct(shape, f32)...  4.76 us

profile of v1, /device:TPU:1, one launch (start us, length us, event | category | flops | bytes accessed | tf_op | source)
XLA Modules:
  0.0 53.8 jit_solution(5293383458570034248)
XLA Ops:
  0.6 48.4 %shard_map.49 = (f32[4,2,2,8,8,8,128]{6,5,4,3,2,1,0:T(8,128)S(1)}, f32[4,2,2,8,8,8,128]{6,5,4,3,2,1,0:T(8,128)S(1)}, f32[2,2,8,8,8,128]{5,4,3,2,1,0:T(8,128)S(1)}, f32[8,128]{1,0:T(8,128)S(1)}) custom-call(f32[4,8,8,8,512]{4,3,2,1,0:T(8,128)} %loads.1, f32[8,8,8,512]{3,2,1,0:T(8,128)} %conduct.1), custom_call_target="tpu_custom_call" | custom-call | tf_op jit(solution)/shard_map/pallas_call | solution.py:587
  49.1 4.8 %shard_map.50 = (f32[4,8,8,8,512]{4,3,2,1,0:T(8,128)}, f32[4,8,8,8,512]{4,3,2,1,0:T(8,128)}, f32[4,8,8,8,512]{4,3,2,1,0:T(8,128)}) custom-call(f32[4,2,2,8,8,8,128]{6,5,4,3,2,1,0:T(8,128)S(1)} %get-tuple-element.7.rhs, f32[4,2,2,8,8,8,128]{6,5,4,3,2,1,0:T(8,128)S(1)} %get-tuple-element.8.image, f32[2,2,8,8,8,128]{5,4,3,2,1,0:T(8,128)S(1)} %get-tuple-element.9.inverse, ...), custom_call_target="tpu_custom_call" | custom-call | tf_op jit(solution)/shard_map/pallas_call | solution.py:616

commit v2 on v1

v2 whole, which is shorter than its diff:
```python
import functools

import jax
import jax.numpy as jnp
import numpy as np
from jax import lax
from jax.experimental import pallas as pl
from jax.experimental.pallas import tpu as pltpu
from jax.sharding import PartitionSpec as P

NODES = 8
SOURCES = 4
LANES = 128
N_ROW = 8
N_COL = 16
SCREENING = 0.5
GLL_INNER = [
    -0.8717401485096066,
    -0.5917001814331423,
    -0.2092992179024789,
    0.2092992179024789,
    0.5917001814331423,
    0.8717401485096066,
]
MESH = pl.DeviceIdType.MESH
FIELD = (2, 2, NODES, NODES, NODES, LANES)


def gll_tables():
    degree = NODES - 1
    points = np.array([-1.0] + GLL_INNER + [1.0])
    previous = points * 0.0 + 1.0
    current = points * 1.0
    for order in range(1, degree):
        following = ((2 * order + 1) * points * current - order * previous) / (order + 1)
        previous = current
        current = following
    weights = 2.0 / (degree * (degree + 1) * current**2)
    spread = points[:, None] - points[None, :]
    index_ids = np.arange(NODES)
    same = index_ids[:, None] == index_ids[None, :]
    safe_spread = np.where(same, 1.0, spread)
    deriv = np.where(same, 0.0, current[:, None] / (current[None, :] * safe_spread))
    corner = degree * (degree + 1) / 4.0
    ends = np.where(index_ids == 0, -corner, np.where(index_ids == degree, corner, 0.0))
    deriv = deriv + np.where(same, ends[None, :], 0.0)
    return deriv, weights


DERIV, WEIGHTS = gll_tables()
SQUARE = DERIV * DERIV
HALF = NODES // 2


def halves(table):
    mirrored = table[:HALF, ::-1][:, :HALF]
    direct = table[:HALF, :HALF]
    plus = (direct + mirrored) / 2.0
    minus = (direct - mirrored) / 2.0
    return plus.tolist(), minus.tolist()


D_PLUS, D_MINUS = halves(DERIV * np.sqrt(2.0))
Q_PLUS, Q_MINUS = halves(SQUARE * 2.0)


def fold(values):
    plus = [values[i] + values[7 - i] for i in range(HALF)]
    minus = [values[i] - values[7 - i] for i in range(HALF)]
    return plus, minus


def combine(table, values, transposed):
    out = []
    for a in range(HALF):
        total = None
        for i in range(HALF):
            factor = table[i][a] if transposed else table[a][i]
            term = values[i] * factor
            total = term if total is None else total + term
        out.append(total)
    return out


def unfold(base, turn):
    low = [base[a] + turn[a] for a in range(HALF)]
    high = [base[a] - turn[a] for a in range(HALF)]
    return low + high[::-1]


def derive(values):
    plus, minus = fold(values)
    return unfold(combine(D_MINUS, minus, False), combine(D_PLUS, plus, False))


def derive_back(values):
    plus, minus = fold(values)
    return unfold(combine(D_PLUS, minus, True), combine(D_MINUS, plus, True))


def square_back(values):
    plus, minus = fold(values)
    return unfold(combine(Q_PLUS, plus, True), combine(Q_MINUS, minus, True))


def tree_sum(terms):
    while len(terms) > 1:
        terms = [a + b for a, b in zip(terms[::2], terms[1::2])]
    return terms[0]


def lines_x(t):
    return [[(t, i, j) for i in range(NODES)] for j in range(NODES)]


def lines_y(g):
    return [[(g, u, j) for j in range(NODES)] for u in range(4)]


def lines_z(g):
    return [[(g, u, pl.ds(k, 8, stride=8)) for k in range(NODES)] for u in range(4)]


def views(ref):
    along_x = ref.reshape(4, NODES, NODES, NODES, LANES)
    along_y = ref.reshape(8, 4, NODES, NODES, LANES)
    along_z = ref.reshape(8, 4, NODES * NODES, LANES)
    return along_x, along_y, along_z


def read(ref, line):
    return [ref[at] for at in line]


def write(ref, line, values):
    for at, value in zip(line, values):
        ref[at] = value


def sum_z(first, last):
    lane = lax.broadcasted_iota(jnp.int32, (8, LANES), 1)
    after = jnp.where(lane < LANES - 1, pltpu.roll(first, LANES - 1, 1), 0.0)
    before = jnp.where(lane > 0, pltpu.roll(last, 1, 1), 0.0)
    return first + before, last + after


def assemble_inside(ref):
    for ey in range(2):
        for j in range(NODES):
            both = ref[0, ey, 7, j] + ref[1, ey, 0, j]
            ref[0, ey, 7, j] = both
            ref[1, ey, 0, j] = both
    for ex in range(2):
        for i in range(NODES):
            both = ref[ex, 0, i, 7] + ref[ex, 1, i, 0]
            ref[ex, 0, i, 7] = both
            ref[ex, 1, i, 0] = both
    strips = views(ref)[2]

    def along_z(g, carry):
        lines = [line for u in range(4) for line in lines_z(g * 4 + u)]
        ends = [(strips[line[0]], strips[line[7]]) for line in lines]
        ends = [sum_z(first, last) for first, last in ends]
        for line, (first, last) in zip(lines, ends):
            strips[line[0]] = first
            strips[line[7]] = last
        return carry

    lax.fori_loop(0, 2, along_z, 0)


DIAG = SOURCES
IMAGE = SOURCES + 1
FIELDS = 2 * SOURCES + 1


def solve_kernel(
    loads,
    conduct,
    fields,
    scalars,
    flux,
    flux_z,
    part_z,
    z0,
    weighted,
    from_x,
    from_y,
    from_edge,
    sums,
    part,
    gather_row,
    gather_col,
    in_sem,
    send_sem,
    recv_sem,
    sum_send,
    sum_recv,
):
    row = lax.axis_index("row")
    col = lax.axis_index("col")
    for ex in range(2):
        for ey in range(2):
            lanes = pl.ds((ex * 2 + ey) * LANES, LANES)
            pltpu.make_async_copy(
                conduct.at[:, :, :, lanes], flux.at[ex, ey], in_sem.at[SOURCES]
            ).start()
    for s in range(SOURCES):
        for ex in range(2):
            for ey in range(2):
                lanes = pl.ds((ex * 2 + ey) * LANES, LANES)
                pltpu.make_async_copy(
                    loads.at[s, :, :, :, lanes], fields.at[s, ex, ey], in_sem.at[s]
                ).start()

    has_up, has_down = row < N_ROW - 1, row > 0
    has_right, has_left = col < N_COL - 1, col > 0
    ways = [
        (1, 0, has_up),
        (-1, 0, has_down),
        (0, 1, has_right),
        (0, -1, has_left),
        (1, 1, has_up & has_right),
        (1, -1, has_up & has_left),
        (-1, 1, has_down & has_right),
        (-1, -1, has_down & has_left),
    ]
    barrier = pltpu.get_barrier_semaphore()
    corners = 0
    for dr, dc, there in ways[4:]:

        @pl.when(there)
        def _():
            pl.semaphore_signal(barrier, 1, device_id=(row + dr, col + dc), device_id_type=MESH)

        corners = corners + there.astype(jnp.int32)
    for step in range(1, N_COL):
        pl.semaphore_signal(
            barrier, 1, device_id=(row, lax.rem(col + step, N_COL)), device_id_type=MESH
        )
    for step in range(1, N_ROW):
        pl.semaphore_signal(
            barrier, 1, device_id=(lax.rem(row + step, N_ROW), col), device_id_type=MESH
        )

    def transfers(q):
        ref = fields.at[q]
        pieces = [
            (ref.at[1, :, 7], from_x.at[q, 0]),
            (ref.at[0, :, 0], from_x.at[q, 1]),
            (ref.at[:, 1, :, 7], from_y.at[q, 0]),
            (ref.at[:, 0, :, 0], from_y.at[q, 1]),
            (ref.at[1, 1, 7, 7], from_edge.at[q, 0]),
            (ref.at[1, 0, 7, 0], from_edge.at[q, 1]),
            (ref.at[0, 1, 0, 7], from_edge.at[q, 2]),
            (ref.at[0, 0, 0, 0], from_edge.at[q, 3]),
        ]
        return [
            pltpu.make_async_remote_copy(
                src,
                dst,
                send_sem.at[q, n],
                recv_sem.at[q, n],
                device_id=(row + ways[n][0], col + ways[n][1]),
                device_id_type=MESH,
            )
            for n, (src, dst) in enumerate(pieces)
        ]

    order = (2, 3, 4, 5, 6, 7, 0, 1)

    def send(q):
        copies = transfers(q)
        for n in order:

            @pl.when(ways[n][2])
            def _():
                copies[n].start()

    def collect(q):
        copies = transfers(q)
        for n in order:

            @pl.when(ways[n][2])
            def _():
                copies[n].wait_send()

        for n in order:

            @pl.when(ways[n ^ 1 if n < 4 else 11 - n][2])
            def _():
                copies[n].wait_recv()

        ref = fields.at[q]
        for ey in range(2):
            for j in range(NODES):
                ref[0, ey, 0, j] = ref[0, ey, 0, j] + from_x[q, 0, ey, j]
                ref[1, ey, 7, j] = ref[1, ey, 7, j] + from_x[q, 1, ey, j]
        for ex in range(2):
            for i in range(NODES):
                ref[ex, 0, i, 0] = ref[ex, 0, i, 0] + from_y[q, 0, ex, i]
                ref[ex, 1, i, 7] = ref[ex, 1, i, 7] + from_y[q, 1, ex, i]
        for corner in range(4):
            ex, ey = corner // 2, corner % 2
            at = (ex, ey, 7 * ex, 7 * ey)
            ref[at] = ref[at] + from_edge[q, corner]

    def clear(ref, there, pick):
        @pl.when(jnp.logical_not(there))
        def _():
            def body(q, carry):
                target = pick(ref, q)
                target[...] = jnp.zeros_like(target)
                return carry

            lax.fori_loop(0, FIELDS, body, 0)

    clear(from_x, has_down, lambda ref, q: ref.at[q, 0])
    clear(from_x, has_up, lambda ref, q: ref.at[q, 1])
    clear(from_y, has_left, lambda ref, q: ref.at[q, 0])
    clear(from_y, has_right, lambda ref, q: ref.at[q, 1])
    clear(from_edge, has_down & has_left, lambda ref, q: ref.at[q, 0])
    clear(from_edge, has_down & has_right, lambda ref, q: ref.at[q, 1])
    clear(from_edge, has_up & has_left, lambda ref, q: ref.at[q, 2])
    clear(from_edge, has_up & has_right, lambda ref, q: ref.at[q, 3])
    sums[...] = jnp.zeros_like(sums)

    flux_v = views(flux)
    flux_zv = views(flux_z)
    part_v = views(part_z)
    z0_v = views(z0)
    weighted_v = views(weighted)
    diag_v = views(fields.at[DIAG])

    pltpu.make_async_copy(flux, flux, in_sem.at[SOURCES]).wait()
    node = lax.broadcasted_iota(jnp.int32, (8, LANES), 0)
    lane = lax.broadcasted_iota(jnp.int32, (8, LANES), 1)
    weight_z = jnp.full((8, LANES), WEIGHTS[3], jnp.float32)
    for k in (0, 1, 2):
        ends = (node == k) | (node == 7 - k)
        weight_z = jnp.where(ends, jnp.float32(WEIGHTS[k]), weight_z)

    def diag_x(t, carry):
        for j, line in enumerate(lines_x(t)):
            values = [
                v * (weight_z * float(SCREENING * WEIGHTS[i] * WEIGHTS[j]))
                for i, v in enumerate(read(flux_v[0], line))
            ]
            write(flux_v[0], line, values)
            write(diag_v[0], line, [r + v for r, v in zip(square_back(values), values)])
        return carry

    def diag_yz(g, carry):
        for line, strip in zip(lines_y(g), lines_z(g)):
            before = read(diag_v[1], line)
            result_y = square_back(read(flux_v[1], line))
            values = read(flux_v[2], strip)
            write(flux_zv[1], line, values)
            write(part_v[2], strip, square_back(values))
            write(diag_v[1], line, [b + r for b, r in zip(before, result_y)])
        return carry

    def diag_sum(g, carry):
        for line in lines_y(g):
            both = zip(read(diag_v[1], line), read(part_v[1], line))
            write(diag_v[1], line, [b + r for b, r in both])
        return carry

    lax.fori_loop(0, 4, diag_x, 0)
    lax.fori_loop(0, 8, diag_yz, 0)
    lax.fori_loop(0, 8, diag_sum, 0)

    def prepare(n, carry):
        q = lax.rem(n + DIAG, DIAG + 1)

        @pl.when(n > 0)
        def _():
            pltpu.make_async_copy(fields.at[q], fields.at[q], in_sem.at[q]).wait()

        assemble_inside(fields.at[q])
        return carry

    lax.fori_loop(0, DIAG + 1, prepare, 0)
    pl.semaphore_wait(barrier, N_ROW - 1 + N_COL - 1 + corners)

    def send_first(n, carry):
        send(lax.rem(n + DIAG, DIAG + 1))
        return carry

    lax.fori_loop(0, DIAG + 1, send_first, 0)

    twice_z = ((node == 0) & (lane > 0)) | ((node == 7) & (lane < LANES - 1))
    share_z = jnp.where(twice_z, jnp.float32(0.5), jnp.float32(1.0))
    zero = jnp.zeros((8, LANES), jnp.float32)

    def put_sum(at, value):
        sums[pl.ds(at, 1), :] = jnp.sum(value, axis=0, keepdims=True)

    def invert_all():
        def invert(g, carry):
            for line in lines_y(g):
                values = [1.0 / v for v in read(diag_v[1], line)]
                write(diag_v[1], line, values)
                write(weighted_v[1], line, [v * share_z for v in values])
            return carry

        lax.fori_loop(0, 8, invert, 0)

        def part_of(there):
            return 0.5 if there is None else jnp.where(there, 0.5, 1.0).astype(jnp.float32)

        for there, ex, i in [(has_down, 0, 0), (None, 0, 7), (None, 1, 0), (has_up, 1, 7)]:
            for ey in range(2):
                weighted[ex, ey, i] = weighted[ex, ey, i] * part_of(there)
        for there, ey, j in [(has_left, 0, 0), (None, 0, 7), (None, 1, 0), (has_right, 1, 7)]:
            for ex in range(2):
                weighted[ex, ey, :, j] = weighted[ex, ey, :, j] * part_of(there)

    def apply(s):
        right_v = views(fields.at[s])
        image_v = views(fields.at[IMAGE + s])

        def scale(g, carry):
            terms = []
            for line in lines_y(g):
                values = read(right_v[1], line)
                write(z0_v[1], line, [v * d for v, d in zip(values, read(diag_v[1], line))])
                terms += [v * v * d for v, d in zip(values, read(weighted_v[1], line))]
            return carry + tree_sum(terms)

        put_sum(s, lax.fori_loop(0, 8, scale, zero))

        def stiff(values, weight):
            return derive_back([g * w for g, w in zip(derive(values), weight)])

        def stiff_x(t, carry):
            for line in lines_x(t):
                values, weight = read(z0_v[0], line), read(flux_v[0], line)
                result = stiff(values, weight)
                write(image_v[0], line, [r + w * v for r, w, v in zip(result, weight, values)])
            return carry

        def stiff_yz(g, carry):
            pairs = list(zip(lines_y(g), lines_z(g)))
            results = [stiff(read(z0_v[2], strip), read(flux_zv[1], line)) for line, strip in pairs]
            for (line, strip), result in zip(pairs, results):
                write(part_v[2], strip, result)
            for line, _ in pairs:
                before = read(image_v[1], line)
                result = stiff(read(z0_v[1], line), read(flux_v[1], line))
                write(image_v[1], line, [b + r for b, r in zip(before, result)])
            return carry

        def add_z(g, carry):
            terms = []
            for line in lines_y(g):
                both = zip(read(image_v[1], line), read(part_v[1], line))
                total = [a + b for a, b in both]
                write(image_v[1], line, total)
                terms += [v * r for v, r in zip(read(z0_v[1], line), total)]
            return carry + tree_sum(terms)

        lax.fori_loop(0, 4, stiff_x, 0)
        lax.fori_loop(0, 8, stiff_yz, 0)
        put_sum(SOURCES + s, lax.fori_loop(0, 8, add_z, zero))
        assemble_inside(fields.at[IMAGE + s])
        send(IMAGE + s)

    def settle(s):
        image_v = views(fields.at[IMAGE + s])

        def square(g, carry):
            terms = []
            for line in lines_y(g):
                both = zip(read(image_v[1], line), read(weighted_v[1], line))
                terms += [v * v * w for v, w in both]
            return carry + tree_sum(terms)

        put_sum(2 * SOURCES + s, lax.fori_loop(0, 8, square, zero))

    def advance(n, carry):
        q = jnp.where(n == 0, DIAG, jnp.where(n <= SOURCES, n - 1, n))
        collect(q)
        pl.when(n == 0)(invert_all)
        pl.when((n > 0) & (n <= SOURCES))(lambda: apply(n - 1))
        pl.when(n > SOURCES)(lambda: settle(n - IMAGE))
        return carry

    lax.fori_loop(0, FIELDS, advance, 0)

    def gather(stage, slots, mine, count, at, target):
        slots[at] = mine[...]
        copies = [
            pltpu.make_async_remote_copy(
                mine,
                slots.at[at],
                sum_send.at[stage],
                sum_recv.at[stage],
                device_id=target(lax.rem(at + step, count)),
                device_id_type=MESH,
            )
            for step in range(1, count)
        ]
        for copy in copies:
            copy.start()
        others = slots.at[pl.ds(0, count - 1)]
        pltpu.make_async_copy(others, others, sum_recv.at[stage]).wait()
        pltpu.make_async_copy(others, others, sum_send.at[stage]).wait()
        total = slots[0]
        for n in range(1, count):
            total = total + slots[n]
        return total

    total = jnp.sum(sums[...], axis=1, keepdims=True)
    node16 = lax.broadcasted_iota(jnp.int32, (16, LANES), 0)
    lane16 = lax.broadcasted_iota(jnp.int32, (16, LANES), 1)
    packed = jnp.where(node16 == lane16, jnp.broadcast_to(total, (16, LANES)), 0.0)
    part[0:1, :] = jnp.sum(packed, axis=0, keepdims=True)
    part[1:2, :] = gather(0, gather_row, part.at[0:1], N_ROW, row, lambda r: (r, col))
    total = gather(1, gather_col, part.at[1:2], N_COL, col, lambda c: (row, c))
    total = jnp.broadcast_to(total, (16, LANES))
    total = jnp.sum(jnp.where(node16 == lane16, total, 0.0), axis=1, keepdims=True)
    rz_first, curvature, square = total[0:4], total[4:8], total[8:12]
    alpha = rz_first / curvature
    rz_second = alpha * alpha * square - rz_first
    beta = rz_second / rz_first
    scalars[0:4, :] = jnp.broadcast_to(alpha, (4, LANES))
    scalars[4:8, :] = jnp.broadcast_to(beta, (4, LANES))


SLOTS = 8


def update_kernel(fields, scalars, first, second, third, staging, sem):
    outputs = (first, second, third)

    def copies(n):
        return [
            pltpu.make_async_copy(
                staging.at[n % SLOTS, q], outputs[q].at[n // NODES, n % NODES], sem.at[n % SLOTS, q]
            )
            for q in range(3)
        ]

    def step(n, carry):
        s, i, slot = n // NODES, n % NODES, n % SLOTS

        @pl.when(n >= SLOTS)
        def _():
            for copy in copies(n - SLOTS):
                copy.wait()

        alpha = jnp.broadcast_to(scalars[pl.ds(s, 1), :], (8, LANES))
        beta = jnp.broadcast_to(scalars[pl.ds(s + 4, 1), :], (8, LANES))
        for ex in range(2):
            for ey in range(2):
                lanes = pl.ds((ex * 2 + ey) * LANES, LANES)
                for j in range(NODES):
                    right = fields[s, ex, ey, i, j]
                    inv = fields[DIAG, ex, ey, i, j]
                    rest = right - alpha * fields[IMAGE + s, ex, ey, i, j]
                    staging[slot, 0, j, :, lanes] = alpha * (right * inv)
                    staging[slot, 1, j, :, lanes] = rest
                    staging[slot, 2, j, :, lanes] = (rest + beta * right) * inv
        for copy in copies(n):
            copy.start()
        return carry

    steps = SOURCES * NODES
    lax.fori_loop(0, steps, step, 0)
    for n in range(steps - SLOTS, steps):
        for copy in copies(n):
            copy.wait()


def per_device(loads, conduct):
    f32 = jnp.float32
    vmem = pltpu.VMEM
    whole = pl.BlockSpec(memory_space=vmem)
    fields, scalars = pl.pallas_call(
        solve_kernel,
        out_shape=[vmem((FIELDS,) + FIELD, f32), vmem((8, LANES), f32)],
        in_specs=[pl.BlockSpec(memory_space=pl.ANY)] * 2,
        out_specs=[whole] * 2,
        scratch_shapes=[
            vmem(FIELD, f32),
            vmem(FIELD, f32),
            vmem(FIELD, f32),
            vmem(FIELD, f32),
            vmem(FIELD, f32),
            vmem((9, 2, 2, NODES, NODES, LANES), f32),
            vmem((9, 2, 2, NODES, NODES, LANES), f32),
            vmem((9, 4, NODES, LANES), f32),
            vmem((16, LANES), f32),
            vmem((8, LANES), f32),
            vmem((N_ROW, 1, LANES), f32),
            vmem((N_COL, 1, LANES), f32),
            pltpu.SemaphoreType.DMA((SOURCES + 1,)),
            pltpu.SemaphoreType.DMA((9, 8)),
            pltpu.SemaphoreType.DMA((9, 8)),
            pltpu.SemaphoreType.DMA((2,)),
            pltpu.SemaphoreType.DMA((2,)),
        ],
        compiler_params=pltpu.CompilerParams(
            collective_id=0, has_side_effects=True, vmem_limit_bytes=40 * 1024 * 1024
        ),
    )(*[pltpu.with_memory_space_constraint(x, pltpu.HBM) for x in (loads, conduct)])
    shape = (SOURCES, NODES, NODES, NODES, 4 * LANES)
    return pl.pallas_call(
        update_kernel,
        out_shape=[jax.ShapeDtypeStruct(shape, f32)] * 3,
        in_specs=[whole] * 2,
        out_specs=[pl.BlockSpec(memory_space=pl.ANY)] * 3,
        scratch_shapes=[
            vmem((SLOTS, 3, NODES, NODES, 4 * LANES), f32),
            pltpu.SemaphoreType.DMA((SLOTS, 3)),
        ],
        compiler_params=pltpu.CompilerParams(vmem_limit_bytes=16 * 1024 * 1024),
    )(*[pltpu.with_memory_space_constraint(x, vmem) for x in (fields, scalars)])


def solution(mesh):
    in_specs = (P(None, None, None, None, ("row", "col")), P(None, None, None, ("row", "col")))
    out = P(None, None, None, None, ("row", "col"))
    return jax.shard_map(
        per_device, mesh=mesh, in_specs=in_specs, out_specs=(out, out, out), check_vma=False
    )
```

time: 54.1 us -> 47.7 us (0.88)
  Pallas kernels: 53.2 us -> 46.8 us
    pallas_call x1, Pallas kernels: 48.4 us -> 42 us  [per_device(): pl.pallas_call(solve_kernel, out_shape=[vmem((FIELDS,) + FIELD, f32), vme...]
where the time goes in v2:
time: 47.7 us; the launch traced here: 47.4 us
  Pallas kernels  46.8 us (98%)
  between operations  0.64 us (1%)
    pallas_call x1, Pallas kernels, per_device(): pl.pallas_call(solve_kernel, out_shape=[vmem((FIELDS,) + FIELD, f32), vme...  42 us
    pallas_call x1, Pallas kernels, per_device(): pl.pallas_call(update_kernel, out_shape=[jax.ShapeDtypeStruct(shape, f32)...  4.76 us

profile of v2, /device:TPU:1, one launch (start us, length us, event | category | flops | bytes accessed | tf_op | source)
XLA Modules:
  0.0 47.4 jit_solution(6144171470531174417)
XLA Ops:
  0.6 42.0 %shard_map.49 = (f32[9,2,2,8,8,8,128]{6,5,4,3,2,1,0:T(8,128)S(1)}, f32[8,128]{1,0:T(8,128)S(1)}) custom-call(f32[4,8,8,8,512]{4,3,2,1,0:T(8,128)} %loads.1, f32[8,8,8,512]{3,2,1,0:T(8,128)} %conduct.1), custom_call_target="tpu_custom_call" | custom-call | tf_op jit(solution)/shard_map/pallas_call | solution.py:580
  42.7 4.8 %shard_map.50 = (f32[4,8,8,8,512]{4,3,2,1,0:T(8,128)}, f32[4,8,8,8,512]{4,3,2,1,0:T(8,128)}, f32[4,8,8,8,512]{4,3,2,1,0:T(8,128)}) custom-call(f32[9,2,2,8,8,8,128]{6,5,4,3,2,1,0:T(8,128)S(1)} %get-tuple-element.5.fields, f32[8,128]{1,0:T(8,128)S(1)} %get-tuple-element.6.scalars), custom_call_target="tpu_custom_call" | custom-call | tf_op jit(solution)/shard_map/pallas_call | solution.py:609

commit v3 on v2

--- a/solution.py
+++ b/solution.py
@@ -60,7 +60,8 @@
     return plus.tolist(), minus.tolist()
 
 
-D_PLUS, D_MINUS = halves(DERIV * np.sqrt(2.0))
+SLOPE = DERIV * np.sqrt(2.0)
+D_PLUS, D_MINUS = halves(SLOPE)
 Q_PLUS, Q_MINUS = halves(SQUARE * 2.0)
 
 
@@ -178,11 +179,15 @@
     loads,
     conduct,
     fields,
+    inverse,
     scalars,
     flux,
     flux_z,
     part_z,
     z0,
+    z_face,
+    coef_x,
+    coef_y,
     weighted,
     from_x,
     from_y,
@@ -245,52 +250,44 @@
 
     def transfers(q):
         ref = fields.at[q]
+        rest = pl.ds(1, NODES - 1)
         pieces = [
-            (ref.at[1, :, 7], from_x.at[q, 0]),
-            (ref.at[0, :, 0], from_x.at[q, 1]),
-            (ref.at[:, 1, :, 7], from_y.at[q, 0]),
-            (ref.at[:, 0, :, 0], from_y.at[q, 1]),
-            (ref.at[1, 1, 7, 7], from_edge.at[q, 0]),
-            (ref.at[1, 0, 7, 0], from_edge.at[q, 1]),
-            (ref.at[0, 1, 0, 7], from_edge.at[q, 2]),
-            (ref.at[0, 0, 0, 0], from_edge.at[q, 3]),
+            (2, ref.at[0, 1, :, 7], from_y.at[q, 0, 0]),
+            (2, ref.at[1, 1, rest, 7], from_y.at[q, 0, 1, rest]),
+            (3, ref.at[0, 0, :, 0], from_y.at[q, 1, 0]),
+            (3, ref.at[1, 0, rest, 0], from_y.at[q, 1, 1, rest]),
+            (4, ref.at[1, 1, 7, 7], from_edge.at[q, 0]),
+            (5, ref.at[1, 0, 7, 0], from_edge.at[q, 1]),
+            (6, ref.at[0, 1, 0, 7], from_edge.at[q, 2]),
+            (7, ref.at[0, 0, 0, 0], from_edge.at[q, 3]),
+            (0, ref.at[1, :, 7], from_x.at[q, 0]),
+            (1, ref.at[0, :, 0], from_x.at[q, 1]),
         ]
         return [
-            pltpu.make_async_remote_copy(
-                src,
-                dst,
-                send_sem.at[q, n],
-                recv_sem.at[q, n],
-                device_id=(row + ways[n][0], col + ways[n][1]),
-                device_id_type=MESH,
+            (
+                way,
+                pltpu.make_async_remote_copy(
+                    src,
+                    dst,
+                    send_sem.at[q, n],
+                    recv_sem.at[q, n],
+                    device_id=(row + ways[way][0], col + ways[way][1]),
+                    device_id_type=MESH,
+                ),
             )
-            for n, (src, dst) in enumerate(pieces)
+            for n, (way, src, dst) in enumerate(pieces)
         ]
 
-    order = (2, 3, 4, 5, 6, 7, 0, 1)
-
     def send(q):
-        copies = transfers(q)
-        for n in order:
-
-            @pl.when(ways[n][2])
-            def _():
-                copies[n].start()
+        for way, copy in transfers(q):
+            pl.when(ways[way][2])(copy.start)
 
     def collect(q):
         copies = transfers(q)
-        for n in order:
-
-            @pl.when(ways[n][2])
-            def _():
-                copies[n].wait_send()
-
-        for n in order:
-
-            @pl.when(ways[n ^ 1 if n < 4 else 11 - n][2])
-            def _():
-                copies[n].wait_recv()
-
+        for way, copy in copies:
+            pl.when(ways[way][2])(copy.wait_send)
+        for way, copy in copies:
+            pl.when(ways[way ^ 1 if way < 4 else 11 - way][2])(copy.wait_recv)
         ref = fields.at[q]
         for ey in range(2):
             for j in range(NODES):
@@ -298,8 +295,9 @@
                 ref[1, ey, 7, j] = ref[1, ey, 7, j] + from_x[q, 1, ey, j]
         for ex in range(2):
             for i in range(NODES):
-                ref[ex, 0, i, 0] = ref[ex, 0, i, 0] + from_y[q, 0, ex, i]
-                ref[ex, 1, i, 7] = ref[ex, 1, i, 7] + from_y[q, 1, ex, i]
+                at = (0, 7) if (ex, i) == (1, 0) else (ex, i)
+                ref[ex, 0, i, 0] = ref[ex, 0, i, 0] + from_y[(q, 0) + at]
+                ref[ex, 1, i, 7] = ref[ex, 1, i, 7] + from_y[(q, 1) + at]
         for corner in range(4):
             ex, ey = corner // 2, corner % 2
             at = (ex, ey, 7 * ex, 7 * ey)
@@ -330,6 +328,7 @@
     part_v = views(part_z)
     z0_v = views(z0)
     weighted_v = views(weighted)
+    inverse_v = views(inverse)
     diag_v = views(fields.at[DIAG])
 
     pltpu.make_async_copy(flux, flux, in_sem.at[SOURCES]).wait()
@@ -381,57 +380,34 @@
         return carry
 
     lax.fori_loop(0, DIAG + 1, prepare, 0)
-    pl.semaphore_wait(barrier, N_ROW - 1 + N_COL - 1 + corners)
-
-    def send_first(n, carry):
-        send(lax.rem(n + DIAG, DIAG + 1))
-        return carry
-
-    lax.fori_loop(0, DIAG + 1, send_first, 0)
-
-    twice_z = ((node == 0) & (lane > 0)) | ((node == 7) & (lane < LANES - 1))
-    share_z = jnp.where(twice_z, jnp.float32(0.5), jnp.float32(1.0))
-    zero = jnp.zeros((8, LANES), jnp.float32)
-
-    def put_sum(at, value):
-        sums[pl.ds(at, 1), :] = jnp.sum(value, axis=0, keepdims=True)
-
-    def invert_all():
-        def invert(g, carry):
-            for line in lines_y(g):
-                values = [1.0 / v for v in read(diag_v[1], line)]
-                write(diag_v[1], line, values)
-                write(weighted_v[1], line, [v * share_z for v in values])
-            return carry
-
-        lax.fori_loop(0, 8, invert, 0)
-
-        def part_of(there):
-            return 0.5 if there is None else jnp.where(there, 0.5, 1.0).astype(jnp.float32)
-
-        for there, ex, i in [(has_down, 0, 0), (None, 0, 7), (None, 1, 0), (has_up, 1, 7)]:
-            for ey in range(2):
-                weighted[ex, ey, i] = weighted[ex, ey, i] * part_of(there)
-        for there, ey, j in [(has_left, 0, 0), (None, 0, 7), (None, 1, 0), (has_right, 1, 7)]:
-            for ex in range(2):
-                weighted[ex, ey, :, j] = weighted[ex, ey, :, j] * part_of(there)
-
-    def apply(s):
+
+    def invert(g, carry):
+        for line in lines_y(g):
+            write(inverse_v[1], line, [1.0 / v for v in read(diag_v[1], line)])
+        return carry
+
+    lax.fori_loop(0, 8, invert, 0)
+
+    def stiff(values, weight):
+        return derive_back([g * w for g, w in zip(derive(values), weight)])
+
+    def own_part(s):
         right_v = views(fields.at[s])
         image_v = views(fields.at[IMAGE + s])
 
         def scale(g, carry):
-            terms = []
             for line in lines_y(g):
-                values = read(right_v[1], line)
-                write(z0_v[1], line, [v * d for v, d in zip(values, read(diag_v[1], line))])
-                terms += [v * v * d for v, d in zip(values, read(weighted_v[1], line))]
-            return carry + tree_sum(terms)
-
-        put_sum(s, lax.fori_loop(0, 8, scale, zero))
-
-        def stiff(values, weight):
-            return derive_back([g * w for g, w in zip(derive(values), weight)])
+                both = zip(read(right_v[1], line), read(inverse_v[1], line))
+                write(z0_v[1], line, [v * d for v, d in both])
+            return carry
+
+        lax.fori_loop(0, 8, scale, 0)
+        empty = jnp.zeros((8, LANES), jnp.float32)
+        for ex in range(2):
+            for ey in range(2):
+                for n in range(NODES):
+                    z0[ex, ey, 7 * ex, n] = empty
+                    z0[ex, ey, n, 7 * ey] = empty
 
         def stiff_x(t, carry):
             for line in lines_x(t):
@@ -441,52 +417,164 @@
             return carry
 
         def stiff_yz(g, carry):
-            pairs = list(zip(lines_y(g), lines_z(g)))
-            results = [stiff(read(z0_v[2], strip), read(flux_zv[1], line)) for line, strip in pairs]
-            for (line, strip), result in zip(pairs, results):
-                write(part_v[2], strip, result)
-            for line, _ in pairs:
+            for line, strip in zip(lines_y(g), lines_z(g)):
                 before = read(image_v[1], line)
-                result = stiff(read(z0_v[1], line), read(flux_v[1], line))
-                write(image_v[1], line, [b + r for b, r in zip(before, result)])
+                result_y = stiff(read(z0_v[1], line), read(flux_v[1], line))
+                result_z = stiff(read(z0_v[2], strip), read(flux_zv[1], line))
+                write(part_v[2], strip, result_z)
+                write(image_v[1], line, [b + r for b, r in zip(before, result_y)])
             return carry
 
         def add_z(g, carry):
-            terms = []
             for line in lines_y(g):
                 both = zip(read(image_v[1], line), read(part_v[1], line))
-                total = [a + b for a, b in both]
-                write(image_v[1], line, total)
-                terms += [v * r for v, r in zip(read(z0_v[1], line), total)]
-            return carry + tree_sum(terms)
+                write(image_v[1], line, [a + b for a, b in both])
+            return carry
 
         lax.fori_loop(0, 4, stiff_x, 0)
         lax.fori_loop(0, 8, stiff_yz, 0)
-        put_sum(SOURCES + s, lax.fori_loop(0, 8, add_z, zero))
-        assemble_inside(fields.at[IMAGE + s])
+        lax.fori_loop(0, 8, add_z, 0)
+
+    def send_first(n, carry):
+        send(lax.rem(n + DIAG, DIAG + 1))
+        return carry
+
+    def begin(s, carry):
+        @pl.when(s == 1)
+        def _():
+            pl.semaphore_wait(barrier, N_ROW - 1 + N_COL - 1 + corners)
+            lax.fori_loop(0, DIAG + 1, send_first, 0)
+
+        own_part(s)
+        return carry
+
+    lax.fori_loop(0, SOURCES, begin, 0)
+
+    for side in range(2):
+        end = 7 * side
+
+        def lean(other, carry):
+            for n in range(NODES):
+                weight = [flux[side, other, a, n] for a in range(NODES)]
+                result = derive_back([w * float(SLOPE[a, end]) for a, w in enumerate(weight)])
+                result[end] = result[end] + weight[end]
+                for i in range(NODES):
+                    coef_x[side, other, i, n] = result[i]
+                weight = [flux[other, side, n, b] for b in range(NODES)]
+                result = derive_back([w * float(SLOPE[b, end]) for b, w in enumerate(weight)])
+                for j in range(NODES):
+                    coef_y[other, side, n, j] = result[j]
+            return carry
+
+        lax.fori_loop(0, 2, lean, 0)
+
+    collect(DIAG)
+    for ex in range(2):
+        for ey in range(2):
+            for n in range(NODES):
+                for at in ((ex, ey, 7 * ex, n), (ex, ey, n, 7 * ey)):
+                    inverse[at] = 1.0 / fields[(DIAG,) + at]
+
+    face_v = views(z_face)[0]
+    face_strip = z_face.reshape(4, NODES, NODES * NODES, LANES)
+    face_flat = z_face.reshape(4, NODES**3, LANES)
+    flux_flat = flux.reshape(4, NODES**3, LANES)
+    coef_xv = views(coef_x)[0]
+    coef_yv = views(coef_y)[0]
+
+    def correct(s, carry):
+        collect(s)
+        for ex in range(2):
+            for ey in range(2):
+                for n in range(NODES):
+                    for at in ((ex, ey, 7 * ex, n), (ex, ey, n, 7 * ey)):
+                        z_face[at] = fields[(s,) + at] * inverse[at]
+        target = fields.at[IMAGE + s]
+        image_v = views(target)[0]
+        image_strip = target.reshape(4, NODES, NODES * NODES, LANES)
+        image_flat = target.reshape(4, NODES**3, LANES)
+
+        def faces(t, carry):
+            i0 = 7 * (t // 2)
+            j0 = 7 * lax.rem(t, 2)
+            nodes = range(NODES)
+            values = [face_v[t, i, j0] for i in nodes]
+            weight = [flux_v[0][t, i, j0] for i in nodes]
+            result = stiff(values, weight)
+            result = [r + w * v for r, w, v in zip(result, weight, values)]
+            result_y = stiff([face_v[t, i0, j] for j in nodes], [flux_v[0][t, i0, j] for j in nodes])
+            strips = [(t, i0, pl.ds(k, 8, stride=8)) for k in nodes]
+            result_z = stiff(read(face_strip, strips), [flux_zv[0][t, i0, k] for k in nodes])
+            columns = [(t, pl.ds(j0 * 8 + k, 8, stride=64)) for k in nodes]
+            values = [jnp.where(node == i0, 0.0, v) for v in read(face_flat, columns)]
+            result_c = stiff(values, read(flux_flat, columns))
+            for at, r in zip(strips, result_z):
+                image_strip[at] = image_strip[at] + r
+            for at, r in zip(columns, result_c):
+                image_flat[at] = image_flat[at] + r
+            for i, r in zip(nodes, result):
+                image_v[t, i, j0] = image_v[t, i, j0] + r
+            for j, r in zip(nodes, result_y):
+                image_v[t, i0, j] = image_v[t, i0, j] + r
+            ends_x = [jnp.where(j0 == j, 0.0, face_v[t, i0, j]) for j in nodes]
+            ends_y = [jnp.where(i0 == i, 0.0, face_v[t, i, j0]) for i in nodes]
+            for i in nodes:
+                for j in nodes:
+                    more = coef_xv[t, i, j] * ends_x[j] + coef_yv[t, i, j] * ends_y[i]
+                    image_v[t, i, j] = image_v[t, i, j] + more
+            return carry
+
+        lax.fori_loop(0, 4, faces, 0)
+        assemble_inside(target)
         send(IMAGE + s)
-
-    def settle(s):
-        image_v = views(fields.at[IMAGE + s])
-
-        def square(g, carry):
-            terms = []
+        return carry
+
+    lax.fori_loop(0, SOURCES, correct, 0)
+
+    twice_z = ((node == 0) & (lane > 0)) | ((node == 7) & (lane < LANES - 1))
+    share_z = jnp.where(twice_z, jnp.float32(0.5), jnp.float32(1.0))
+
+    def share(g, carry):
+        for line in lines_y(g):
+            write(weighted_v[1], line, [v * share_z for v in read(inverse_v[1], line)])
+        return carry
+
+    lax.fori_loop(0, 8, share, 0)
+
+    def part_of(there):
+        return 0.5 if there is None else jnp.where(there, 0.5, 1.0).astype(jnp.float32)
+
+    for there, ex, i in [(has_down, 0, 0), (None, 0, 7), (None, 1, 0), (has_up, 1, 7)]:
+        for ey in range(2):
+            weighted[ex, ey, i] = weighted[ex, ey, i] * part_of(there)
+    for there, ey, j in [(has_left, 0, 0), (None, 0, 7), (None, 1, 0), (has_right, 1, 7)]:
+        for ex in range(2):
+            weighted[ex, ey, :, j] = weighted[ex, ey, :, j] * part_of(there)
+
+    zero = jnp.zeros((8, LANES), jnp.float32)
+
+    def settle(s, carry):
+        collect(IMAGE + s)
+        right_v = views(fields.at[s])[1]
+        image_v = views(fields.at[IMAGE + s])[1]
+
+        def products(g, carry):
+            terms = [[], [], []]
             for line in lines_y(g):
-                both = zip(read(image_v[1], line), read(weighted_v[1], line))
-                terms += [v * v * w for v, w in both]
-            return carry + tree_sum(terms)
-
-        put_sum(2 * SOURCES + s, lax.fori_loop(0, 8, square, zero))
-
-    def advance(n, carry):
-        q = jnp.where(n == 0, DIAG, jnp.where(n <= SOURCES, n - 1, n))
-        collect(q)
-        pl.when(n == 0)(invert_all)
-        pl.when((n > 0) & (n <= SOURCES))(lambda: apply(n - 1))
-        pl.when(n > SOURCES)(lambda: settle(n - IMAGE))
-        return carry
-
-    lax.fori_loop(0, FIELDS, advance, 0)
+                for at in line:
+                    r, v, w = right_v[at], image_v[at], weighted_v[1][at]
+                    rw = r * w
+                    terms[0].append(r * rw)
+                    terms[1].append(v * rw)
+                    terms[2].append(v * (v * w))
+            return tuple(c + tree_sum(t) for c, t in zip(carry, terms))
+
+        totals = lax.fori_loop(0, 8, products, (zero, zero, zero))
+        for n, total in enumerate(totals):
+            sums[pl.ds(n * SOURCES + s, 1), :] = jnp.sum(total, axis=0, keepdims=True)
+        return carry
+
+    lax.fori_loop(0, SOURCES, settle, 0)
 
     def gather(stage, slots, mine, count, at, target):
         slots[at] = mine[...]
@@ -531,7 +619,7 @@
 SLOTS = 8
 
 
-def update_kernel(fields, scalars, first, second, third, staging, sem):
+def update_kernel(fields, inverse, scalars, first, second, third, staging, sem):
     outputs = (first, second, third)
 
     def copies(n):
@@ -557,7 +645,7 @@
                 lanes = pl.ds((ex * 2 + ey) * LANES, LANES)
                 for j in range(NODES):
                     right = fields[s, ex, ey, i, j]
-                    inv = fields[DIAG, ex, ey, i, j]
+                    inv = inverse[ex, ey, i, j]
                     rest = right - alpha * fields[IMAGE + s, ex, ey, i, j]
                     staging[slot, 0, j, :, lanes] = alpha * (right * inv)
                     staging[slot, 1, j, :, lanes] = rest
@@ -577,27 +665,23 @@
     f32 = jnp.float32
     vmem = pltpu.VMEM
     whole = pl.BlockSpec(memory_space=vmem)
-    fields, scalars = pl.pallas_call(
+    results = pl.pallas_call(
         solve_kernel,
-        out_shape=[vmem((FIELDS,) + FIELD, f32), vmem((8, LANES), f32)],
+        out_shape=[vmem((FIELDS,) + FIELD, f32), vmem(FIELD, f32), vmem((8, LANES), f32)],
         in_specs=[pl.BlockSpec(memory_space=pl.ANY)] * 2,
-        out_specs=[whole] * 2,
-        scratch_shapes=[
-            vmem(FIELD, f32),
-            vmem(FIELD, f32),
-            vmem(FIELD, f32),
-            vmem(FIELD, f32),
-            vmem(FIELD, f32),
-            vmem((9, 2, 2, NODES, NODES, LANES), f32),
-            vmem((9, 2, 2, NODES, NODES, LANES), f32),
-            vmem((9, 4, NODES, LANES), f32),
+        out_specs=[whole] * 3,
+        scratch_shapes=[vmem(FIELD, f32)] * 8
+        + [
+            vmem((FIELDS, 2, 2, NODES, NODES, LANES), f32),
+            vmem((FIELDS, 2, 2, NODES, NODES, LANES), f32),
+            vmem((FIELDS, 4, NODES, LANES), f32),
             vmem((16, LANES), f32),
             vmem((8, LANES), f32),
             vmem((N_ROW, 1, LANES), f32),
             vmem((N_COL, 1, LANES), f32),
             pltpu.SemaphoreType.DMA((SOURCES + 1,)),
-            pltpu.SemaphoreType.DMA((9, 8)),
-            pltpu.SemaphoreType.DMA((9, 8)),
+            pltpu.SemaphoreType.DMA((FIELDS, 10)),
+            pltpu.SemaphoreType.DMA((FIELDS, 10)),
             pltpu.SemaphoreType.DMA((2,)),
             pltpu.SemaphoreType.DMA((2,)),
         ],
@@ -609,14 +693,14 @@
     return pl.pallas_call(
         update_kernel,
         out_shape=[jax.ShapeDtypeStruct(shape, f32)] * 3,
-        in_specs=[whole] * 2,
+        in_specs=[whole] * 3,
         out_specs=[pl.BlockSpec(memory_space=pl.ANY)] * 3,
         scratch_shapes=[
             vmem((SLOTS, 3, NODES, NODES, 4 * LANES), f32),
             pltpu.SemaphoreType.DMA((SLOTS, 3)),
         ],
         compiler_params=pltpu.CompilerParams(vmem_limit_bytes=16 * 1024 * 1024),
-    )(*[pltpu.with_memory_space_constraint(x, vmem) for x in (fields, scalars)])
+    )(*[pltpu.with_memory_space_constraint(x, vmem) for x in results])
 
 
 def solution(mesh):

time: 47.7 us -> 45.5 us (0.954)
  Pallas kernels: 46.8 us -> 44.6 us
    pallas_call x1, Pallas kernels: 42 us -> 39.9 us  [per_device(): pl.pallas_call(solve_kernel, out_shape=[vmem((FIELDS,) + FIELD, f32), vme...]
where the time goes in v3:
time: 45.5 us; the launch traced here: 45.3 us
  Pallas kernels  44.6 us (98%)
  between operations  0.64 us (1%)
    pallas_call x1, Pallas kernels, per_device(): pl.pallas_call(solve_kernel, out_shape=[vmem((FIELDS,) + FIELD, f32), vme...  39.9 us
    pallas_call x1, Pallas kernels, per_device(): pl.pallas_call(update_kernel, out_shape=[jax.ShapeDtypeStruct(shape, f32)...  4.76 us

profile of v3, /device:TPU:1, one launch (start us, length us, event | category | flops | bytes accessed | tf_op | source)
XLA Modules:
  0.0 45.3 jit_solution(15826543335856232941)
XLA Ops:
  0.6 39.9 %shard_map.49 = (f32[9,2,2,8,8,8,128]{6,5,4,3,2,1,0:T(8,128)S(1)}, f32[2,2,8,8,8,128]{5,4,3,2,1,0:T(8,128)S(1)}, f32[8,128]{1,0:T(8,128)S(1)}) custom-call(f32[4,8,8,8,512]{4,3,2,1,0:T(8,128)} %loads.1, f32[8,8,8,512]{3,2,1,0:T(8,128)} %conduct.1), custom_call_target="tpu_custom_call" | custom-call | tf_op jit(solution)/shard_map/pallas_call | solution.py:668
  40.5 4.8 %shard_map.50 = (f32[4,8,8,8,512]{4,3,2,1,0:T(8,128)}, f32[4,8,8,8,512]{4,3,2,1,0:T(8,128)}, f32[4,8,8,8,512]{4,3,2,1,0:T(8,128)}) custom-call(f32[9,2,2,8,8,8,128]{6,5,4,3,2,1,0:T(8,128)S(1)} %get-tuple-element.6.fields, f32[2,2,8,8,8,128]{5,4,3,2,1,0:T(8,128)S(1)} %get-tuple-element.7.inverse, f32[8,128]{1,0:T(8,128)S(1)} %get-tuple-element.8.scalars), custom_call_target="tpu_custom_call" | custom-call | tf_op jit(solution)/shard_map/pallas_call | solution.py:693

commit v4 on v3

--- a/solution.py
+++ b/solution.py
@@ -230,6 +230,8 @@
         (-1, 1, has_down & has_right),
         (-1, -1, has_down & has_left),
     ]
+    sides_x = has_up.astype(jnp.int32) + has_down.astype(jnp.int32)
+    sides_y = has_right.astype(jnp.int32) + has_left.astype(jnp.int32)
     barrier = pltpu.get_barrier_semaphore()
     corners = 0
     for dr, dc, there in ways[4:]:
@@ -269,13 +271,13 @@
                 pltpu.make_async_remote_copy(
                     src,
                     dst,
-                    send_sem.at[q, n],
-                    recv_sem.at[q, n],
+                    send_sem.at[q],
+                    recv_sem.at[q],
                     device_id=(row + ways[way][0], col + ways[way][1]),
                     device_id_type=MESH,
                 ),
             )
-            for n, (way, src, dst) in enumerate(pieces)
+            for way, src, dst in pieces
         ]
 
     def send(q):
@@ -283,12 +285,17 @@
             pl.when(ways[way][2])(copy.start)
 
     def collect(q):
-        copies = transfers(q)
-        for way, copy in copies:
-            pl.when(ways[way][2])(copy.wait_send)
-        for way, copy in copies:
-            pl.when(ways[way ^ 1 if way < 4 else 11 - way][2])(copy.wait_recv)
         ref = fields.at[q]
+        tiles = ref.reshape(4 * NODES * NODES, NODES, LANES)
+        for across in (1, 2):
+            for along in (1, 2):
+
+                @pl.when((sides_x == across) & (sides_y == along))
+                def _():
+                    size = tiles.at[pl.ds(0, 16 * across + 15 * along + across * along)]
+                    pltpu.make_async_copy(size, size, send_sem.at[q]).wait()
+                    pltpu.make_async_copy(size, size, recv_sem.at[q]).wait()
+
         for ey in range(2):
             for j in range(NODES):
                 ref[0, ey, 0, j] = ref[0, ey, 0, j] + from_x[q, 0, ey, j]
@@ -386,7 +393,8 @@
             write(inverse_v[1], line, [1.0 / v for v in read(diag_v[1], line)])
         return carry
 
-    lax.fori_loop(0, 8, invert, 0)
+    z0_strip = z0.reshape(4, NODES, NODES * NODES, LANES)
+    part_strip = part_z.reshape(4, NODES, NODES * NODES, LANES)
 
     def stiff(values, weight):
         return derive_back([g * w for g, w in zip(derive(values), weight)])
@@ -409,42 +417,54 @@
                     z0[ex, ey, 7 * ex, n] = empty
                     z0[ex, ey, n, 7 * ey] = empty
 
+        def stiff_z(t, carry):
+            planes = pl.ds(1 - t // 2, NODES - 1)
+            values, weight = z0_strip.at[t, planes], flux_zv[0].at[t, planes]
+            result = part_strip.at[t, planes]
+            for u in range(NODES - 1):
+                strips = [(u, pl.ds(k, 8, stride=8)) for k in range(NODES)]
+                out = stiff(read(values, strips), [weight[u, k] for k in range(NODES)])
+                write(result, strips, out)
+            return carry
+
         def stiff_x(t, carry):
-            for line in lines_x(t):
-                values, weight = read(z0_v[0], line), read(flux_v[0], line)
-                result = stiff(values, weight)
-                write(image_v[0], line, [r + w * v for r, w, v in zip(result, weight, values)])
+            end = lax.rem(t, 2)
+            lines = pl.ds(1 - end, NODES - 1)
+            values, weight = z0_v[0].at[t, :, lines], flux_v[0].at[t, :, lines]
+            result = image_v[0].at[t, :, lines]
+            for n in range(NODES - 1):
+                line = [(i, n) for i in range(NODES)]
+                v, w = read(values, line), read(weight, line)
+                out = stiff(v, w)
+                write(result, line, [r + b * a for r, b, a in zip(out, w, v)])
+            for i in range(NODES):
+                image_v[0][t, i, 7 * end] = empty
             return carry
 
-        def stiff_yz(g, carry):
-            for line, strip in zip(lines_y(g), lines_z(g)):
-                before = read(image_v[1], line)
-                result_y = stiff(read(z0_v[1], line), read(flux_v[1], line))
-                result_z = stiff(read(z0_v[2], strip), read(flux_zv[1], line))
-                write(part_v[2], strip, result_z)
-                write(image_v[1], line, [b + r for b, r in zip(before, result_y)])
+        def stiff_y(t, carry):
+            planes = pl.ds(1 - t // 2, NODES - 1)
+            values, weight = z0_v[0].at[t, planes], flux_v[0].at[t, planes]
+            result, other = image_v[0].at[t, planes], part_v[0].at[t, planes]
+            for u in range(NODES - 1):
+                line = [(u, j) for j in range(NODES)]
+                out = stiff(read(values, line), read(weight, line))
+                before = zip(read(result, line), read(other, line), out)
+                write(result, line, [a + b + r for a, b, r in before])
             return carry
 
-        def add_z(g, carry):
-            for line in lines_y(g):
-                both = zip(read(image_v[1], line), read(part_v[1], line))
-                write(image_v[1], line, [a + b for a, b in both])
-            return carry
-
+        lax.fori_loop(0, 4, stiff_z, 0)
         lax.fori_loop(0, 4, stiff_x, 0)
-        lax.fori_loop(0, 8, stiff_yz, 0)
-        lax.fori_loop(0, 8, add_z, 0)
+        lax.fori_loop(0, 4, stiff_y, 0)
 
     def send_first(n, carry):
         send(lax.rem(n + DIAG, DIAG + 1))
         return carry
 
+    pl.semaphore_wait(barrier, N_ROW - 1 + N_COL - 1 + corners)
+    lax.fori_loop(0, DIAG + 1, send_first, 0)
+    lax.fori_loop(0, 8, invert, 0)
+
     def begin(s, carry):
-        @pl.when(s == 1)
-        def _():
-            pl.semaphore_wait(barrier, N_ROW - 1 + N_COL - 1 + corners)
-            lax.fori_loop(0, DIAG + 1, send_first, 0)
-
         own_part(s)
         return carry
 
@@ -625,18 +645,20 @@
     def copies(n):
         return [
             pltpu.make_async_copy(
-                staging.at[n % SLOTS, q], outputs[q].at[n // NODES, n % NODES], sem.at[n % SLOTS, q]
+                staging.at[n % SLOTS, q], outputs[q].at[n // NODES, n % NODES], sem.at[n % SLOTS]
             )
             for q in range(3)
         ]
 
+    def await_slot(slot):
+        pltpu.make_async_copy(staging.at[slot], staging.at[slot], sem.at[slot]).wait()
+
     def step(n, carry):
         s, i, slot = n // NODES, n % NODES, n % SLOTS
 
         @pl.when(n >= SLOTS)
         def _():
-            for copy in copies(n - SLOTS):
-                copy.wait()
+            await_slot(slot)
 
         alpha = jnp.broadcast_to(scalars[pl.ds(s, 1), :], (8, LANES))
         beta = jnp.broadcast_to(scalars[pl.ds(s + 4, 1), :], (8, LANES))
@@ -657,8 +679,7 @@
     steps = SOURCES * NODES
     lax.fori_loop(0, steps, step, 0)
     for n in range(steps - SLOTS, steps):
-        for copy in copies(n):
-            copy.wait()
+        await_slot(n % SLOTS)
 
 
 def per_device(loads, conduct):
@@ -680,8 +701,8 @@
             vmem((N_ROW, 1, LANES), f32),
             vmem((N_COL, 1, LANES), f32),
             pltpu.SemaphoreType.DMA((SOURCES + 1,)),
-            pltpu.SemaphoreType.DMA((FIELDS, 10)),
-            pltpu.SemaphoreType.DMA((FIELDS, 10)),
+            pltpu.SemaphoreType.DMA((FIELDS,)),
+            pltpu.SemaphoreType.DMA((FIELDS,)),
             pltpu.SemaphoreType.DMA((2,)),
             pltpu.SemaphoreType.DMA((2,)),
         ],
@@ -697,7 +718,7 @@
         out_specs=[pl.BlockSpec(memory_space=pl.ANY)] * 3,
         scratch_shapes=[
             vmem((SLOTS, 3, NODES, NODES, 4 * LANES), f32),
-            pltpu.SemaphoreType.DMA((SLOTS, 3)),
+            pltpu.SemaphoreType.DMA((SLOTS,)),
         ],
         compiler_params=pltpu.CompilerParams(vmem_limit_bytes=16 * 1024 * 1024),
     )(*[pltpu.with_memory_space_constraint(x, vmem) for x in results])

time: 45.5 us -> 42.7 us (0.938)
  Pallas kernels: 44.6 us -> 41.8 us
    pallas_call x1, Pallas kernels: 39.9 us -> 37.2 us  [per_device(): pl.pallas_call(solve_kernel, out_shape=[vmem((FIELDS,) + FIELD, f32), vme...]
where the time goes in v4:
time: 42.7 us; the launch traced here: 42.4 us
  Pallas kernels  41.8 us (98%)
  between operations  0.64 us (1%)
    pallas_call x1, Pallas kernels, per_device(): pl.pallas_call(solve_kernel, out_shape=[vmem((FIELDS,) + FIELD, f32), vme...  37.2 us
    pallas_call x1, Pallas kernels, per_device(): pl.pallas_call(update_kernel, out_shape=[jax.ShapeDtypeStruct(shape, f32)...  4.61 us

profile of v4, /device:TPU:1, one launch (start us, length us, event | category | flops | bytes accessed | tf_op | source)
XLA Modules:
  0.0 42.4 jit_solution(17383542157118896007)
XLA Ops:
  0.6 37.2 %shard_map.49 = (f32[9,2,2,8,8,8,128]{6,5,4,3,2,1,0:T(8,128)S(1)}, f32[2,2,8,8,8,128]{5,4,3,2,1,0:T(8,128)S(1)}, f32[8,128]{1,0:T(8,128)S(1)}) custom-call(f32[4,8,8,8,512]{4,3,2,1,0:T(8,128)} %loads.1, f32[8,8,8,512]{3,2,1,0:T(8,128)} %conduct.1), custom_call_target="tpu_custom_call" | custom-call | tf_op jit(solution)/shard_map/pallas_call | solution.py:689
  37.8 4.6 %shard_map.50 = (f32[4,8,8,8,512]{4,3,2,1,0:T(8,128)}, f32[4,8,8,8,512]{4,3,2,1,0:T(8,128)}, f32[4,8,8,8,512]{4,3,2,1,0:T(8,128)}) custom-call(f32[9,2,2,8,8,8,128]{6,5,4,3,2,1,0:T(8,128)S(1)} %get-tuple-element.6.fields, f32[2,2,8,8,8,128]{5,4,3,2,1,0:T(8,128)S(1)} %get-tuple-element.7.inverse, f32[8,128]{1,0:T(8,128)S(1)} %get-tuple-element.8.scalars), custom_call_target="tpu_custom_call" | custom-call | tf_op jit(solution)/shard_map/pallas_call | solution.py:714

commit v5 on v4

--- a/solution.py
+++ b/solution.py
@@ -194,13 +194,13 @@
     from_edge,
     sums,
     part,
-    gather_row,
-    gather_col,
+    gathered,
     in_sem,
     send_sem,
     recv_sem,
     sum_send,
     sum_recv,
+    ready,
 ):
     row = lax.axis_index("row")
     col = lax.axis_index("col")
@@ -462,6 +462,14 @@
 
     pl.semaphore_wait(barrier, N_ROW - 1 + N_COL - 1 + corners)
     lax.fori_loop(0, DIAG + 1, send_first, 0)
+
+    def tell(step, carry):
+        pl.semaphore_signal(
+            ready, 1, device_id=(row, lax.rem(col + step, N_COL)), device_id_type=MESH
+        )
+        return carry
+
+    lax.fori_loop(1, N_COL, tell, 0)
     lax.fori_loop(0, 8, invert, 0)
 
     def begin(s, carry):
@@ -596,36 +604,34 @@
 
     lax.fori_loop(0, SOURCES, settle, 0)
 
-    def gather(stage, slots, mine, count, at, target):
-        slots[at] = mine[...]
-        copies = [
-            pltpu.make_async_remote_copy(
-                mine,
-                slots.at[at],
-                sum_send.at[stage],
-                sum_recv.at[stage],
-                device_id=target(lax.rem(at + step, count)),
-                device_id_type=MESH,
-            )
-            for step in range(1, count)
-        ]
-        for copy in copies:
-            copy.start()
-        others = slots.at[pl.ds(0, count - 1)]
-        pltpu.make_async_copy(others, others, sum_recv.at[stage]).wait()
-        pltpu.make_async_copy(others, others, sum_send.at[stage]).wait()
-        total = slots[0]
-        for n in range(1, count):
-            total = total + slots[n]
-        return total
-
     total = jnp.sum(sums[...], axis=1, keepdims=True)
     node16 = lax.broadcasted_iota(jnp.int32, (16, LANES), 0)
     lane16 = lax.broadcasted_iota(jnp.int32, (16, LANES), 1)
     packed = jnp.where(node16 == lane16, jnp.broadcast_to(total, (16, LANES)), 0.0)
-    part[0:1, :] = jnp.sum(packed, axis=0, keepdims=True)
-    part[1:2, :] = gather(0, gather_row, part.at[0:1], N_ROW, row, lambda r: (r, col))
-    total = gather(1, gather_col, part.at[1:2], N_COL, col, lambda c: (row, c))
+    packed = jnp.sum(packed, axis=0, keepdims=True)
+    part[0:1, :] = packed
+    mine = pl.ds(row * N_COL + col, 1)
+    gathered[mine, :] = packed
+    pl.semaphore_wait(ready, N_COL - 1)
+
+    def spread(step, carry):
+        there = (lax.rem(row + step // N_COL, N_ROW), lax.rem(col + lax.rem(step, N_COL), N_COL))
+        pltpu.make_async_remote_copy(
+            part.at[0:1],
+            gathered.at[mine],
+            sum_send.at[0],
+            sum_recv.at[0],
+            device_id=there,
+            device_id_type=MESH,
+        ).start()
+        return carry
+
+    lax.fori_loop(1, N_ROW * N_COL, spread, 0)
+    others = gathered.at[pl.ds(0, N_ROW * N_COL - 1)]
+    pltpu.make_async_copy(others, others, sum_recv.at[0]).wait()
+    pltpu.make_async_copy(others, others, sum_send.at[0]).wait()
+    total = tree_sum([gathered[pl.ds(8 * n, 8), :] for n in range(N_ROW * N_COL // 8)])
+    total = jnp.sum(total, axis=0, keepdims=True)
     total = jnp.broadcast_to(total, (16, LANES))
     total = jnp.sum(jnp.where(node16 == lane16, total, 0.0), axis=1, keepdims=True)
     rz_first, curvature, square = total[0:4], total[4:8], total[8:12]
@@ -698,13 +704,13 @@
             vmem((FIELDS, 4, NODES, LANES), f32),
             vmem((16, LANES), f32),
             vmem((8, LANES), f32),
-            vmem((N_ROW, 1, LANES), f32),
-            vmem((N_COL, 1, LANES), f32),
+            vmem((N_ROW * N_COL, LANES), f32),
             pltpu.SemaphoreType.DMA((SOURCES + 1,)),
             pltpu.SemaphoreType.DMA((FIELDS,)),
             pltpu.SemaphoreType.DMA((FIELDS,)),
-            pltpu.SemaphoreType.DMA((2,)),
-            pltpu.SemaphoreType.DMA((2,)),
+            pltpu.SemaphoreType.DMA((1,)),
+            pltpu.SemaphoreType.DMA((1,)),
+            pltpu.SemaphoreType.REGULAR,
         ],
         compiler_params=pltpu.CompilerParams(
             collective_id=0, has_side_effects=True, vmem_limit_bytes=40 * 1024 * 1024

time: 42.7 us -> 43 us (level)
  Pallas kernels: 41.8 us -> 42.3 us
    pallas_call x1, Pallas kernels: 37.2 us -> 37.7 us  [per_device(): pl.pallas_call(solve_kernel, out_shape=[vmem((FIELDS,) + FIELD, f32), vme...]
where the time goes in v5:
time: 43 us; the launch traced here: 42.9 us
  Pallas kernels  42.3 us (98%)
  between operations  0.64 us (1%)
    pallas_call x1, Pallas kernels, per_device(): pl.pallas_call(solve_kernel, out_shape=[vmem((FIELDS,) + FIELD, f32), vme...  37.7 us
    pallas_call x1, Pallas kernels, per_device(): pl.pallas_call(update_kernel, out_shape=[jax.ShapeDtypeStruct(shape, f32)...  4.61 us

profile of v5, /device:TPU:1, one launch (start us, length us, event | category | flops | bytes accessed | tf_op | source)
XLA Modules:
  0.0 42.9 jit_solution(17811788597003990898)
XLA Ops:
  0.6 37.7 %shard_map.49 = (f32[9,2,2,8,8,8,128]{6,5,4,3,2,1,0:T(8,128)S(1)}, f32[2,2,8,8,8,128]{5,4,3,2,1,0:T(8,128)S(1)}, f32[8,128]{1,0:T(8,128)S(1)}) custom-call(f32[4,8,8,8,512]{4,3,2,1,0:T(8,128)} %loads.1, f32[8,8,8,512]{3,2,1,0:T(8,128)} %conduct.1), custom_call_target="tpu_custom_call" | custom-call | tf_op jit(solution)/shard_map/pallas_call | solution.py:695
  38.3 4.6 %shard_map.50 = (f32[4,8,8,8,512]{4,3,2,1,0:T(8,128)}, f32[4,8,8,8,512]{4,3,2,1,0:T(8,128)}, f32[4,8,8,8,512]{4,3,2,1,0:T(8,128)}) custom-call(f32[9,2,2,8,8,8,128]{6,5,4,3,2,1,0:T(8,128)S(1)} %get-tuple-element.6.fields, f32[2,2,8,8,8,128]{5,4,3,2,1,0:T(8,128)S(1)} %get-tuple-element.7.inverse, f32[8,128]{1,0:T(8,128)S(1)} %get-tuple-element.8.scalars), custom_call_target="tpu_custom_call" | custom-call | tf_op jit(solution)/shard_map/pallas_call | solution.py:720

commit v6 on v4

--- a/solution.py
+++ b/solution.py
@@ -138,10 +138,10 @@
         ref[at] = value
 
 
-def sum_z(first, last):
+def sum_z(first, last, rows=True):
     lane = lax.broadcasted_iota(jnp.int32, (8, LANES), 1)
-    after = jnp.where(lane < LANES - 1, pltpu.roll(first, LANES - 1, 1), 0.0)
-    before = jnp.where(lane > 0, pltpu.roll(last, 1, 1), 0.0)
+    after = jnp.where((lane < LANES - 1) & rows, pltpu.roll(first, LANES - 1, 1), 0.0)
+    before = jnp.where((lane > 0) & rows, pltpu.roll(last, 1, 1), 0.0)
     return first + before, last + after
 
 
@@ -284,18 +284,19 @@
         for way, copy in transfers(q):
             pl.when(ways[way][2])(copy.start)
 
-    def collect(q):
-        ref = fields.at[q]
-        tiles = ref.reshape(4 * NODES * NODES, NODES, LANES)
+    def await_all(q, sem):
+        tiles = fields.at[q].reshape(4 * NODES * NODES, NODES, LANES)
         for across in (1, 2):
             for along in (1, 2):
 
                 @pl.when((sides_x == across) & (sides_y == along))
                 def _():
                     size = tiles.at[pl.ds(0, 16 * across + 15 * along + across * along)]
-                    pltpu.make_async_copy(size, size, send_sem.at[q]).wait()
-                    pltpu.make_async_copy(size, size, recv_sem.at[q]).wait()
-
+                    pltpu.make_async_copy(size, size, sem).wait()
+
+    def collect(q):
+        await_all(q, recv_sem.at[q])
+        ref = fields.at[q]
         for ey in range(2):
             for j in range(NODES):
                 ref[0, ey, 0, j] = ref[0, ey, 0, j] + from_x[q, 0, ey, j]
@@ -394,14 +395,14 @@
         return carry
 
     z0_strip = z0.reshape(4, NODES, NODES * NODES, LANES)
-    part_strip = part_z.reshape(4, NODES, NODES * NODES, LANES)
 
     def stiff(values, weight):
         return derive_back([g * w for g, w in zip(derive(values), weight)])
 
-    def own_part(s):
+    empty = jnp.zeros((8, LANES), jnp.float32)
+
+    def inside_part(s):
         right_v = views(fields.at[s])
-        image_v = views(fields.at[IMAGE + s])
 
         def scale(g, carry):
             for line in lines_y(g):
@@ -410,22 +411,15 @@
             return carry
 
         lax.fori_loop(0, 8, scale, 0)
-        empty = jnp.zeros((8, LANES), jnp.float32)
         for ex in range(2):
             for ey in range(2):
                 for n in range(NODES):
                     z0[ex, ey, 7 * ex, n] = empty
                     z0[ex, ey, n, 7 * ey] = empty
 
-        def stiff_z(t, carry):
-            planes = pl.ds(1 - t // 2, NODES - 1)
-            values, weight = z0_strip.at[t, planes], flux_zv[0].at[t, planes]
-            result = part_strip.at[t, planes]
-            for u in range(NODES - 1):
-                strips = [(u, pl.ds(k, 8, stride=8)) for k in range(NODES)]
-                out = stiff(read(values, strips), [weight[u, k] for k in range(NODES)])
-                write(result, strips, out)
-            return carry
+    def begin(s, carry):
+        inside_part(s)
+        image_v = views(fields.at[IMAGE + s])
 
         def stiff_x(t, carry):
             end = lax.rem(t, 2)
@@ -444,17 +438,46 @@
         def stiff_y(t, carry):
             planes = pl.ds(1 - t // 2, NODES - 1)
             values, weight = z0_v[0].at[t, planes], flux_v[0].at[t, planes]
-            result, other = image_v[0].at[t, planes], part_v[0].at[t, planes]
+            result = image_v[0].at[t, planes]
             for u in range(NODES - 1):
                 line = [(u, j) for j in range(NODES)]
                 out = stiff(read(values, line), read(weight, line))
-                before = zip(read(result, line), read(other, line), out)
-                write(result, line, [a + b + r for a, b, r in before])
+                write(result, line, [a + r for a, r in zip(read(result, line), out)])
             return carry
 
-        lax.fori_loop(0, 4, stiff_z, 0)
         lax.fori_loop(0, 4, stiff_x, 0)
         lax.fori_loop(0, 4, stiff_y, 0)
+        return carry
+
+    def finish_z(s):
+        inside_part(s)
+        target = fields.at[IMAGE + s]
+        strip = target.reshape(4, NODES, NODES * NODES, LANES)
+
+        def stiff_z(t, carry):
+            planes = pl.ds(1 - t // 2, NODES - 1)
+            values, weight = z0_strip.at[t, planes], flux_zv[0].at[t, planes]
+            result = strip.at[t, planes]
+            off_face = node != 7 * lax.rem(t, 2)
+            for u in range(NODES - 1):
+                strips = [(u, pl.ds(k, 8, stride=8)) for k in range(NODES)]
+                out = stiff(read(values, strips), [weight[u, k] for k in range(NODES)])
+                out = [a + r for a, r in zip(read(result, strips), out)]
+                out[0], out[7] = sum_z(out[0], out[7], off_face)
+                write(result, strips, out)
+            return carry
+
+        lax.fori_loop(0, 4, stiff_z, 0)
+        for ey in range(2):
+            for j in range(1 - ey, NODES - ey):
+                both = target[0, ey, 7, j] + target[1, ey, 0, j]
+                target[0, ey, 7, j] = both
+                target[1, ey, 0, j] = both
+        for ex in range(2):
+            for i in range(1 - ex, NODES - ex):
+                both = target[ex, 0, i, 7] + target[ex, 1, i, 0]
+                target[ex, 0, i, 7] = both
+                target[ex, 1, i, 0] = both
 
     def send_first(n, carry):
         send(lax.rem(n + DIAG, DIAG + 1))
@@ -463,10 +486,6 @@
     pl.semaphore_wait(barrier, N_ROW - 1 + N_COL - 1 + corners)
     lax.fori_loop(0, DIAG + 1, send_first, 0)
     lax.fori_loop(0, 8, invert, 0)
-
-    def begin(s, carry):
-        own_part(s)
-        return carry
 
     lax.fori_loop(0, SOURCES, begin, 0)
 
@@ -488,6 +507,7 @@
 
         lax.fori_loop(0, 2, lean, 0)
 
+    await_all(DIAG, send_sem.at[DIAG])
     collect(DIAG)
     for ex in range(2):
         for ey in range(2):
@@ -503,6 +523,7 @@
     coef_yv = views(coef_y)[0]
 
     def correct(s, carry):
+        await_all(s, send_sem.at[s])
         collect(s)
         for ex in range(2):
             for ey in range(2):
@@ -545,7 +566,23 @@
             return carry
 
         lax.fori_loop(0, 4, faces, 0)
-        assemble_inside(target)
+        for ey in range(2):
+            both = target[0, ey, 7, 7 * ey] + target[1, ey, 0, 7 * ey]
+            target[0, ey, 7, 7 * ey] = both
+            target[1, ey, 0, 7 * ey] = both
+        for ex in range(2):
+            both = target[ex, 0, 7 * ex, 7] + target[ex, 1, 7 * ex, 0]
+            target[ex, 0, 7 * ex, 7] = both
+            target[ex, 1, 7 * ex, 0] = both
+        ends = []
+        for t in range(4):
+            i0, j0 = 7 * (t // 2), 7 * (t % 2)
+            strips = [(t, i0, pl.ds(k, 8, stride=8)) for k in (0, 7)]
+            columns = [(t, pl.ds(j0 * 8 + k, 8, stride=64)) for k in (0, 7)]
+            ends.append((image_strip, strips, read(image_strip, strips)))
+            ends.append((image_flat, columns, read(image_flat, columns)))
+        for ref, at, (first, last) in ends:
+            write(ref, at, sum_z(first, last))
         send(IMAGE + s)
         return carry
 
@@ -574,6 +611,8 @@
     zero = jnp.zeros((8, LANES), jnp.float32)
 
     def settle(s, carry):
+        await_all(IMAGE + s, send_sem.at[IMAGE + s])
+        finish_z(s)
         collect(IMAGE + s)
         right_v = views(fields.at[s])[1]
         image_v = views(fields.at[IMAGE + s])[1]

time: 42.7 us -> 41.3 us (0.967)
  Pallas kernels: 41.8 us -> 40.4 us
    pallas_call x1, Pallas kernels: 37.2 us -> 35.8 us  [per_device(): pl.pallas_call(solve_kernel, out_shape=[vmem((FIELDS,) + FIELD, f32), vme...]
where the time goes in v6:
time: 41.3 us; the launch traced here: 41.1 us
  Pallas kernels  40.4 us (98%)
  between operations  0.64 us (2%)
    pallas_call x1, Pallas kernels, per_device(): pl.pallas_call(solve_kernel, out_shape=[vmem((FIELDS,) + FIELD, f32), vme...  35.8 us
    pallas_call x1, Pallas kernels, per_device(): pl.pallas_call(update_kernel, out_shape=[jax.ShapeDtypeStruct(shape, f32)...  4.61 us

profile of v6, /device:TPU:1, one launch (start us, length us, event | category | flops | bytes accessed | tf_op | source)
XLA Modules:
  0.0 41.1 jit_solution(1031789193056902543)
XLA Ops:
  0.6 35.8 %shard_map.49 = (f32[9,2,2,8,8,8,128]{6,5,4,3,2,1,0:T(8,128)S(1)}, f32[2,2,8,8,8,128]{5,4,3,2,1,0:T(8,128)S(1)}, f32[8,128]{1,0:T(8,128)S(1)}) custom-call(f32[4,8,8,8,512]{4,3,2,1,0:T(8,128)} %loads.1, f32[8,8,8,512]{3,2,1,0:T(8,128)} %conduct.1), custom_call_target="tpu_custom_call" | custom-call | tf_op jit(solution)/shard_map/pallas_call | solution.py:728
  36.4 4.6 %shard_map.50 = (f32[4,8,8,8,512]{4,3,2,1,0:T(8,128)}, f32[4,8,8,8,512]{4,3,2,1,0:T(8,128)}, f32[4,8,8,8,512]{4,3,2,1,0:T(8,128)}) custom-call(f32[9,2,2,8,8,8,128]{6,5,4,3,2,1,0:T(8,128)S(1)} %get-tuple-element.6.fields, f32[2,2,8,8,8,128]{5,4,3,2,1,0:T(8,128)S(1)} %get-tuple-element.7.inverse, f32[8,128]{1,0:T(8,128)S(1)} %get-tuple-element.8.scalars), custom_call_target="tpu_custom_call" | custom-call | tf_op jit(solution)/shard_map/pallas_call | solution.py:753

commit v7 on v6

--- a/solution.py
+++ b/solution.py
@@ -334,7 +334,6 @@
     flux_v = views(flux)
     flux_zv = views(flux_z)
     part_v = views(part_z)
-    z0_v = views(z0)
     weighted_v = views(weighted)
     inverse_v = views(inverse)
     diag_v = views(fields.at[DIAG])
@@ -385,6 +384,12 @@
             pltpu.make_async_copy(fields.at[q], fields.at[q], in_sem.at[q]).wait()
 
         assemble_inside(fields.at[q])
+
+        @pl.when(n == 0)
+        def _():
+            pl.semaphore_wait(barrier, N_ROW - 1 + N_COL - 1 + corners)
+
+        send(q)
         return carry
 
     lax.fori_loop(0, DIAG + 1, prepare, 0)
@@ -394,7 +399,6 @@
             write(inverse_v[1], line, [1.0 / v for v in read(diag_v[1], line)])
         return carry
 
-    z0_strip = z0.reshape(4, NODES, NODES * NODES, LANES)
 
     def stiff(values, weight):
         return derive_back([g * w for g, w in zip(derive(values), weight)])
@@ -403,6 +407,7 @@
 
     def inside_part(s):
         right_v = views(fields.at[s])
+        z0_v = views(z0.at[s])
 
         def scale(g, carry):
             for line in lines_y(g):
@@ -414,11 +419,12 @@
         for ex in range(2):
             for ey in range(2):
                 for n in range(NODES):
-                    z0[ex, ey, 7 * ex, n] = empty
-                    z0[ex, ey, n, 7 * ey] = empty
+                    z0[s, ex, ey, 7 * ex, n] = empty
+                    z0[s, ex, ey, n, 7 * ey] = empty
 
     def begin(s, carry):
         inside_part(s)
+        z0_v = views(z0.at[s])
         image_v = views(fields.at[IMAGE + s])
 
         def stiff_x(t, carry):
@@ -450,7 +456,7 @@
         return carry
 
     def finish_z(s):
-        inside_part(s)
+        z0_strip = z0.at[s].reshape(4, NODES, NODES * NODES, LANES)
         target = fields.at[IMAGE + s]
         strip = target.reshape(4, NODES, NODES * NODES, LANES)
 
@@ -479,12 +485,6 @@
                 target[ex, 0, i, 7] = both
                 target[ex, 1, i, 0] = both
 
-    def send_first(n, carry):
-        send(lax.rem(n + DIAG, DIAG + 1))
-        return carry
-
-    pl.semaphore_wait(barrier, N_ROW - 1 + N_COL - 1 + corners)
-    lax.fori_loop(0, DIAG + 1, send_first, 0)
     lax.fori_loop(0, 8, invert, 0)
 
     lax.fori_loop(0, SOURCES, begin, 0)
@@ -652,19 +652,18 @@
             copy.start()
         others = slots.at[pl.ds(0, count - 1)]
         pltpu.make_async_copy(others, others, sum_recv.at[stage]).wait()
-        pltpu.make_async_copy(others, others, sum_send.at[stage]).wait()
-        total = slots[0]
-        for n in range(1, count):
-            total = total + slots[n]
-        return total
+        return tree_sum([slots[n] for n in range(count)]), others
 
     total = jnp.sum(sums[...], axis=1, keepdims=True)
     node16 = lax.broadcasted_iota(jnp.int32, (16, LANES), 0)
     lane16 = lax.broadcasted_iota(jnp.int32, (16, LANES), 1)
     packed = jnp.where(node16 == lane16, jnp.broadcast_to(total, (16, LANES)), 0.0)
     part[0:1, :] = jnp.sum(packed, axis=0, keepdims=True)
-    part[1:2, :] = gather(0, gather_row, part.at[0:1], N_ROW, row, lambda r: (r, col))
-    total = gather(1, gather_col, part.at[1:2], N_COL, col, lambda c: (row, c))
+    total, sent = gather(0, gather_row, part.at[0:1], N_ROW, row, lambda r: (r, col))
+    part[1:2, :] = total
+    total, sent_too = gather(1, gather_col, part.at[1:2], N_COL, col, lambda c: (row, c))
+    pltpu.make_async_copy(sent, sent, sum_send.at[0]).wait()
+    pltpu.make_async_copy(sent_too, sent_too, sum_send.at[1]).wait()
     total = jnp.broadcast_to(total, (16, LANES))
     total = jnp.sum(jnp.where(node16 == lane16, total, 0.0), axis=1, keepdims=True)
     rz_first, curvature, square = total[0:4], total[4:8], total[8:12]
@@ -730,7 +729,9 @@
         out_shape=[vmem((FIELDS,) + FIELD, f32), vmem(FIELD, f32), vmem((8, LANES), f32)],
         in_specs=[pl.BlockSpec(memory_space=pl.ANY)] * 2,
         out_specs=[whole] * 3,
-        scratch_shapes=[vmem(FIELD, f32)] * 8
+        scratch_shapes=[vmem(FIELD, f32)] * 3
+        + [vmem((SOURCES,) + FIELD, f32)]
+        + [vmem(FIELD, f32)] * 4
         + [
             vmem((FIELDS, 2, 2, NODES, NODES, LANES), f32),
             vmem((FIELDS, 2, 2, NODES, NODES, LANES), f32),

time: 41.3 us -> 41.1 us (level)
  no operation moved by 1% of the time
where the time goes in v7:
time: 41.1 us; the launch traced here: 40.8 us
  Pallas kernels  40.2 us (98%)
  between operations  0.64 us (2%)
    pallas_call x1, Pallas kernels, per_device(): pl.pallas_call(solve_kernel, out_shape=[vmem((FIELDS,) + FIELD, f32), vme...  35.6 us
    pallas_call x1, Pallas kernels, per_device(): pl.pallas_call(update_kernel, out_shape=[jax.ShapeDtypeStruct(shape, f32)...  4.61 us

profile of v7, /device:TPU:1, one launch (start us, length us, event | category | flops | bytes accessed | tf_op | source)
XLA Modules:
  0.0 40.8 jit_solution(6313331323290955077)
XLA Ops:
  0.6 35.6 %shard_map.49 = (f32[9,2,2,8,8,8,128]{6,5,4,3,2,1,0:T(8,128)S(1)}, f32[2,2,8,8,8,128]{5,4,3,2,1,0:T(8,128)S(1)}, f32[8,128]{1,0:T(8,128)S(1)}) custom-call(f32[4,8,8,8,512]{4,3,2,1,0:T(8,128)} %loads.1, f32[8,8,8,512]{3,2,1,0:T(8,128)} %conduct.1), custom_call_target="tpu_custom_call" | custom-call | tf_op jit(solution)/shard_map/pallas_call | solution.py:727
  36.2 4.6 %shard_map.50 = (f32[4,8,8,8,512]{4,3,2,1,0:T(8,128)}, f32[4,8,8,8,512]{4,3,2,1,0:T(8,128)}, f32[4,8,8,8,512]{4,3,2,1,0:T(8,128)}) custom-call(f32[9,2,2,8,8,8,128]{6,5,4,3,2,1,0:T(8,128)S(1)} %get-tuple-element.6.fields, f32[2,2,8,8,8,128]{5,4,3,2,1,0:T(8,128)S(1)} %get-tuple-element.7.inverse, f32[8,128]{1,0:T(8,128)S(1)} %get-tuple-element.8.scalars), custom_call_target="tpu_custom_call" | custom-call | tf_op jit(solution)/shard_map/pallas_call | solution.py:754

commit v8 on v7

--- a/solution.py
+++ b/solution.py
@@ -376,6 +376,24 @@
     lax.fori_loop(0, 8, diag_yz, 0)
     lax.fori_loop(0, 8, diag_sum, 0)
 
+    for side in range(2):
+        end = 7 * side
+
+        def lean(other, carry):
+            for n in range(NODES):
+                weight = [flux[side, other, a, n] for a in range(NODES)]
+                result = derive_back([w * float(SLOPE[a, end]) for a, w in enumerate(weight)])
+                result[end] = result[end] + weight[end]
+                for i in range(NODES):
+                    coef_x[side, other, i, n] = result[i]
+                weight = [flux[other, side, n, b] for b in range(NODES)]
+                result = derive_back([w * float(SLOPE[b, end]) for b, w in enumerate(weight)])
+                for j in range(NODES):
+                    coef_y[other, side, n, j] = result[j]
+            return carry
+
+        lax.fori_loop(0, 2, lean, 0)
+
     def prepare(n, carry):
         q = lax.rem(n + DIAG, DIAG + 1)
 
@@ -488,24 +506,6 @@
     lax.fori_loop(0, 8, invert, 0)
 
     lax.fori_loop(0, SOURCES, begin, 0)
-
-    for side in range(2):
-        end = 7 * side
-
-        def lean(other, carry):
-            for n in range(NODES):
-                weight = [flux[side, other, a, n] for a in range(NODES)]
-                result = derive_back([w * float(SLOPE[a, end]) for a, w in enumerate(weight)])
-                result[end] = result[end] + weight[end]
-                for i in range(NODES):
-                    coef_x[side, other, i, n] = result[i]
-                weight = [flux[other, side, n, b] for b in range(NODES)]
-                result = derive_back([w * float(SLOPE[b, end]) for b, w in enumerate(weight)])
-                for j in range(NODES):
-                    coef_y[other, side, n, j] = result[j]
-            return carry
-
-        lax.fori_loop(0, 2, lean, 0)
 
     await_all(DIAG, send_sem.at[DIAG])
     collect(DIAG)

time: 41.1 us -> 40.6 us (0.988)
  Pallas kernels: 40.2 us -> 39.7 us
    pallas_call x1, Pallas kernels: 35.6 us -> 35.1 us  [per_device(): pl.pallas_call(solve_kernel, out_shape=[vmem((FIELDS,) + FIELD, f32), vme...]
where the time goes in v8:
time: 40.6 us; the launch traced here: 40.4 us
  Pallas kernels  39.7 us (98%)
  between operations  0.64 us (2%)
    pallas_call x1, Pallas kernels, per_device(): pl.pallas_call(solve_kernel, out_shape=[vmem((FIELDS,) + FIELD, f32), vme...  35.1 us
    pallas_call x1, Pallas kernels, per_device(): pl.pallas_call(update_kernel, out_shape=[jax.ShapeDtypeStruct(shape, f32)...  4.61 us

profile of v8, /device:TPU:1, one launch (start us, length us, event | category | flops | bytes accessed | tf_op | source)
XLA Modules:
  0.0 40.4 jit_solution(3876505721428985362)
XLA Ops:
  0.6 35.1 %shard_map.49 = (f32[9,2,2,8,8,8,128]{6,5,4,3,2,1,0:T(8,128)S(1)}, f32[2,2,8,8,8,128]{5,4,3,2,1,0:T(8,128)S(1)}, f32[8,128]{1,0:T(8,128)S(1)}) custom-call(f32[4,8,8,8,512]{4,3,2,1,0:T(8,128)} %loads.1, f32[8,8,8,512]{3,2,1,0:T(8,128)} %conduct.1), custom_call_target="tpu_custom_call" | custom-call | tf_op jit(solution)/shard_map/pallas_call | solution.py:727
  35.8 4.6 %shard_map.50 = (f32[4,8,8,8,512]{4,3,2,1,0:T(8,128)}, f32[4,8,8,8,512]{4,3,2,1,0:T(8,128)}, f32[4,8,8,8,512]{4,3,2,1,0:T(8,128)}) custom-call(f32[9,2,2,8,8,8,128]{6,5,4,3,2,1,0:T(8,128)S(1)} %get-tuple-element.6.fields, f32[2,2,8,8,8,128]{5,4,3,2,1,0:T(8,128)S(1)} %get-tuple-element.7.inverse, f32[8,128]{1,0:T(8,128)S(1)} %get-tuple-element.8.scalars), custom_call_target="tpu_custom_call" | custom-call | tf_op jit(solution)/shard_map/pallas_call | solution.py:754

commit v9 on v8

--- a/solution.py
+++ b/solution.py
@@ -610,9 +610,14 @@
 
     zero = jnp.zeros((8, LANES), jnp.float32)
 
-    def settle(s, carry):
+    def complete(s, carry):
         await_all(IMAGE + s, send_sem.at[IMAGE + s])
         finish_z(s)
+        return carry
+
+    lax.fori_loop(0, SOURCES, complete, 0)
+
+    def settle(s, carry):
         collect(IMAGE + s)
         right_v = views(fields.at[s])[1]
         image_v = views(fields.at[IMAGE + s])[1]

time: 40.6 us -> 40.6 us (level)
  no operation moved by 1% of the time
where the time goes in v9:
time: 40.6 us; the launch traced here: 40.4 us
  Pallas kernels  39.7 us (98%)
  between operations  0.64 us (2%)
    pallas_call x1, Pallas kernels, per_device(): pl.pallas_call(solve_kernel, out_shape=[vmem((FIELDS,) + FIELD, f32), vme...  35.1 us
    pallas_call x1, Pallas kernels, per_device(): pl.pallas_call(update_kernel, out_shape=[jax.ShapeDtypeStruct(shape, f32)...  4.61 us

profile of v9, /device:TPU:1, one launch (start us, length us, event | category | flops | bytes accessed | tf_op | source)
XLA Modules:
  0.0 40.4 jit_solution(17101032648939016686)
XLA Ops:
  0.6 35.1 %shard_map.49 = (f32[9,2,2,8,8,8,128]{6,5,4,3,2,1,0:T(8,128)S(1)}, f32[2,2,8,8,8,128]{5,4,3,2,1,0:T(8,128)S(1)}, f32[8,128]{1,0:T(8,128)S(1)}) custom-call(f32[4,8,8,8,512]{4,3,2,1,0:T(8,128)} %loads.1, f32[8,8,8,512]{3,2,1,0:T(8,128)} %conduct.1), custom_call_target="tpu_custom_call" | custom-call | tf_op jit(solution)/shard_map/pallas_call | solution.py:732
  35.8 4.6 %shard_map.50 = (f32[4,8,8,8,512]{4,3,2,1,0:T(8,128)}, f32[4,8,8,8,512]{4,3,2,1,0:T(8,128)}, f32[4,8,8,8,512]{4,3,2,1,0:T(8,128)}) custom-call(f32[9,2,2,8,8,8,128]{6,5,4,3,2,1,0:T(8,128)S(1)} %get-tuple-element.6.fields, f32[2,2,8,8,8,128]{5,4,3,2,1,0:T(8,128)S(1)} %get-tuple-element.7.inverse, f32[8,128]{1,0:T(8,128)S(1)} %get-tuple-element.8.scalars), custom_call_target="tpu_custom_call" | custom-call | tf_op jit(solution)/shard_map/pallas_call | solution.py:759
